TPU v7x, 128 devices: a whole 4x4x4 slice. The times are simulated.
128 devices in a mesh: aper: 16 (over y, x_hi, core), swath: 8 (over z, x_lo).
Axes of the slice: x: 4 (x_hi: 2, x_lo: 2; x = x_hi * 2 + x_lo), y: 4, z: 4, core: 2. Of those that a mesh axis runs over, the one named last changes fastest.
Arguments:
- polar_field: float32 [2, 2048, 8192], P(None, 'aper', 'swath'), may hold values from -6 to 6
- tap_index: int32 [3, 16, 2, 8, 128], P(None, 'aper'), may hold values from 0 to 127
- tap_weight: float32 [3, 16, 2, 8, 128], P(None, 'aper'), may hold values from -1.5 to 1.5
- range_shift: float32 [3, 16, 2, 128], P(None, 'aper'), may hold values from -8 to 8
- range_gain: float32 [3, 8192], P(None, 'swath'), may hold values from 0.1 to 1.9
- tile_owner: int32 [16, 8, 8, 1], P('aper', 'swath'), may hold values from 0 to 15; in each aligned block of 8 rows (0 to 7, 8 to 15, ..., all dimensions but the last counted through in order) at most 2 rows name the same one
- block_weights: float32 [16, 8, 8, 128, 128], P('aper', 'swath'), may hold values from -0.5 to 0.5
- kernel_index: int32 [16, 8], P('aper', 'swath'), may hold values from 0 to 15
- kernel_bank: float32 [16, 81], replicated, may hold values from -0.625 to 0.625
Outputs:
- deconvolved: float32 [2, 2048, 1024], P(None, 'aper', 'swath')
Inputs may be any that keep to these rules, and one draw needn't show every extreme that they name: `tile_owner`: the 8 polar blocks of one device name any one owner at most 2 times, and some device names one owner exactly 2 times; every owner is named somewhere.
All inputs are finite; a program needn't handle non-finite values.
Results may differ from a plain program's by a relative error of at most 0.00011.
Values sent between devices are 32-bit elements; how exact they have to be, the bound alone decides.
No kernel may reach another device: no remote copies, remote signals or barrier semaphores. Data moves between devices by JAX's collectives and lax.ppermute only.
A program may use at most 128 MiB of HBM per device.

v0:
```python
import math

import jax
import jax.numpy as jnp
from jax import lax
from jax.sharding import PartitionSpec as P

ANGLES = 128
RANGE_BINS = 1024
SECTIONS = 3
BLOCK_BINS = 128
TILE_ROWS = 128
KERNELS = 16


HIGHEST_PRECISION = lax.Precision.HIGHEST


def from_partner(value, axis, apart):
    mask = 2**apart
    pairs = [(source, source ^ mask) for source in range(lax.axis_size(axis))]
    return lax.ppermute(value, axis, pairs)


def extended(cells, sides, width):
    for axis, dim in sides:
        count = lax.axis_size(axis)
        ends = count - 1
        head = lax.slice_in_dim(cells, 0, width, axis=dim)
        tail = lax.slice_in_dim(cells, cells.shape[dim] - width, cells.shape[dim], axis=dim)
        cells = jnp.concatenate(
            [
                lax.ppermute(tail, axis, [(i, (i + 1) % count) for i in range(ends)]),
                cells,
                lax.ppermute(head, axis, [((i + 1) % count, i) for i in range(ends)]),
            ],
            axis=dim,
        )
    return cells


def transform_tables(length):
    bin_index = jnp.arange(length, dtype=jnp.int32)
    product = bin_index[:, None] * bin_index[None, :] % length
    phase_angle = product.astype(jnp.float32) * jnp.float32(2.0 * math.pi / length)
    return (jnp.cos(phase_angle), jnp.sin(phase_angle))


def forward(signal, cos_table, sin_table):
    with_cos = jnp.dot(
        signal, cos_table, precision=HIGHEST_PRECISION, preferred_element_type=jnp.float32
    )
    with_sin = jnp.dot(
        signal, sin_table, precision=HIGHEST_PRECISION, preferred_element_type=jnp.float32
    )
    return jnp.stack([with_cos[0] + with_sin[1], with_cos[1] - with_sin[0]])


def inverse(signal, cos_table, sin_table):
    length = cos_table.shape[0]
    with_cos = jnp.dot(
        signal, cos_table, precision=HIGHEST_PRECISION, preferred_element_type=jnp.float32
    )
    with_sin = jnp.dot(
        signal, sin_table, precision=HIGHEST_PRECISION, preferred_element_type=jnp.float32
    )
    return jnp.stack([(with_cos[0] - with_sin[1]) / length, (with_cos[1] + with_sin[0]) / length])


def interp_matrix(tap_rows, weight_rows, length):
    columns = jnp.arange(length, dtype=jnp.int32)
    matches = (tap_rows[..., None] == columns).astype(jnp.float32)
    return jnp.sum(weight_rows[..., None] * matches, axis=-3)


def phase_tables(shift_rows, length):
    bin_index = jnp.arange(length, dtype=jnp.int32)
    signed = jnp.where(bin_index < length // 2, bin_index, bin_index - length).astype(jnp.float32)
    phase_angle = shift_rows[..., None] * signed * jnp.float32(-2.0 * math.pi / length)
    return (jnp.cos(phase_angle), jnp.sin(phase_angle))


def steer(matrix, shift_rows, spectrum):
    mixed = jnp.einsum(
        "kj,pjr->pkr",
        matrix,
        spectrum,
        precision=HIGHEST_PRECISION,
        preferred_element_type=jnp.float32,
    )
    cos_phase, sin_phase = phase_tables(shift_rows, spectrum.shape[2])
    return jnp.stack(
        [cos_phase * mixed[0] - sin_phase * mixed[1], cos_phase * mixed[1] + sin_phase * mixed[0]]
    )


def shards(
    polar_field,
    tap_index,
    tap_weight,
    range_shift,
    range_gain,
    tile_owner,
    block_weights,
    kernel_index,
    kernel_bank,
):
    cos_table, sin_table = transform_tables(RANGE_BINS)
    position = lax.axis_index("aper")
    current = polar_field
    for merge_step in range(SECTIONS):
        is_upper = position // 2**merge_step % 2 == 1
        matrices = interp_matrix(tap_index[merge_step, 0], tap_weight[merge_step, 0], ANGLES)
        own_matrix = jnp.where(is_upper, matrices[1], matrices[0])
        other_matrix = jnp.where(is_upper, matrices[0], matrices[1])
        own_shift = jnp.where(
            is_upper, range_shift[merge_step, 0, 1], range_shift[merge_step, 0, 0]
        )
        other_shift = jnp.where(
            is_upper, range_shift[merge_step, 0, 0], range_shift[merge_step, 0, 1]
        )
        partner = from_partner(current, "aper", merge_step)
        own_spec = forward(current, cos_table, sin_table)
        other_spec = forward(partner, cos_table, sin_table)
        merged = steer(own_matrix, own_shift, own_spec) + steer(
            other_matrix, other_shift, other_spec
        )
        current = inverse(merged, cos_table, sin_table) * range_gain[merge_step][None, None, :]
    blocks_dev = RANGE_BINS // BLOCK_BINS
    pieces = current.reshape(2, ANGLES, blocks_dev, BLOCK_BINS)
    contrib = jnp.einsum(
        "bxa,pabr->bpxr",
        block_weights[0, 0],
        pieces,
        precision=HIGHEST_PRECISION,
        preferred_element_type=jnp.float32,
    )
    flat_contrib = contrib.reshape(blocks_dev, 2 * TILE_ROWS * BLOCK_BINS)
    owner_row = tile_owner[0, 0, :, 0]
    peers = lax.axis_size("aper")
    targets = jnp.arange(peers, dtype=jnp.int32)
    owner_hits = (owner_row[None, :] == targets[:, None]).astype(jnp.float32)
    outgoing = jnp.dot(
        owner_hits, flat_contrib, precision=HIGHEST_PRECISION, preferred_element_type=jnp.float32
    )
    incoming = lax.all_to_all(outgoing, "aper", split_axis=0, concat_axis=0, tiled=True)
    tile_sum = jnp.sum(incoming, axis=0).reshape(2, TILE_ROWS, BLOCK_BINS)
    padded = extended(tile_sum, (("aper", 1), ("swath", 2)), 4)
    chosen = (kernel_index[0, 0] == jnp.arange(KERNELS, dtype=jnp.int32)).astype(jnp.float32)
    kernel_row = jnp.dot(
        chosen, kernel_bank, precision=HIGHEST_PRECISION, preferred_element_type=jnp.float32
    )
    result_sum = jnp.zeros((2, TILE_ROWS, BLOCK_BINS), jnp.float32)
    for offset in range(81):
        row_shift = offset // 9
        col_shift = offset % 9
        result_sum = (
            result_sum
            + kernel_row[offset]
            * padded[:, row_shift : row_shift + TILE_ROWS, col_shift : col_shift + BLOCK_BINS]
        )
    return result_sum


def solution(mesh):
    in_specs = (
        P(None, "aper", "swath"),
        P(None, "aper", None, None, None),
        P(None, "aper", None, None, None),
        P(None, "aper", None, None),
        P(None, "swath"),
        P("aper", "swath", None, None),
        P("aper", "swath", None, None, None),
        P("aper", "swath"),
        P(),
    )
    out_specs = P(None, "aper", "swath")
    return jax.shard_map(shards, mesh=mesh, in_specs=in_specs, out_specs=out_specs, check_vma=False)
```

profile of v0, /device:TPU:39, one launch (start us, length us, event | category | flops | bytes accessed | tf_op | source)
XLA Modules:
  0.0 524.2 jit_solution(6532144619466249627)
XLA Ops:
  0.7 23.2 %fusion.62 = f32[2,128,1024]{1,2,0:T(8,128)S(1)} fusion(f32[2,128,1024]{2,1,0:T(8,128)} %param.9), kind=kOutput, calls=%fused_computation.48 | convolution fusion | flops 3235905536 | bytes 2097152 | tf_op jit(solution)/shard_map/dot_general | solution.py:50
  26.2 22.6 %fusion.68 = f32[2,128,1024]{1,2,0:T(8,128)S(1)} fusion(f32[2,128,1024]{2,1,0:T(8,128)S(1)} %copy-done.7), kind=kOutput, calls=%fused_computation.50 | convolution fusion | flops 3235905536 | bytes 2097152 | tf_op jit(solution)/shard_map/dot_general | solution.py:53
  50.0 23.1 %fusion.65 = f32[2,128,1024]{1,2,0:T(8,128)S(1)} fusion(f32[2,128,1024]{2,1,0:T(8,128)} %collective-permute-done), kind=kOutput, calls=%fused_computation.49 | convolution fusion | flops 3235905536 | bytes 2097152 | tf_op jit(solution)/shard_map/dot_general | solution.py:50
  73.2 23.4 %fusion.71 = f32[2,128,1024]{1,2,0:T(8,128)S(1)} fusion(f32[2,128,1024]{2,1,0:T(8,128)} %collective-permute-done), kind=kOutput, calls=%fused_computation.51 | convolution fusion | flops 3235905536 | bytes 2097152 | tf_op jit(solution)/shard_map/dot_general | solution.py:53
  102.4 19.1 %fusion.33 = f32[2,128,1024]{2,1,0:T(8,128)S(1)} fusion(f32[1,128,1024]{1,2,0:T(8,128)S(1)} %get-tuple-element.54, f32[1,128,1024]{1,2,0:T(8,128)S(1)} %get-tuple-element.55, f32[1,128,1024]{1,2,0:T(8,128)S(1)} %get-tuple-element.32, f32[1,128,1024]{1,2,0:T(8,128)S(1)} %get-tuple-element.31), kind=kOutput, calls=%fused_computation.37 | convolution fusion | flops 3236691968 | bytes 3145728 | tf_op jit(solution)/shard_map/dot_general | solution.py:61
  121.5 19.7 %fusion.15 = f32[2,128,1024]{2,1,0:T(8,128)S(1)} fusion(f32[1,128,1024]{1,2,0:T(8,128)S(1)} %get-tuple-element.54, f32[1,128,1024]{1,2,0:T(8,128)S(1)} %get-tuple-element.55, f32[1,128,1024]{1,2,0:T(8,128)S(1)} %get-tuple-element.32, f32[1,128,1024]{1,2,0:T(8,128)S(1)} %get-tuple-element.31), kind=kOutput, calls=%fused_computation.19 | convolution fusion | flops 3236691968 | bytes 3145728 | tf_op jit(solution)/shard_map/dot_general | solution.py:64
  141.5 20.1 %fusion.13 = f32[2,128,1024]{2,1,0:T(8,128)S(1)} fusion(f32[2,128,1024]{2,1,0:T(8,128)S(1)} %maximum_multiply_fusion), kind=kOutput, calls=%fused_computation.17 | convolution fusion | flops 3235905536 | bytes 2097152 | tf_op jit(solution)/shard_map/dot_general | solution.py:53
  162.8 20.2 %fusion.31 = f32[2,128,1024]{2,1,0:T(8,128)S(1)} fusion(f32[2,128,1024]{2,1,0:T(8,128)S(1)} %maximum_multiply_fusion), kind=kOutput, calls=%fused_computation.35 | convolution fusion | flops 3235905536 | bytes 2097152 | tf_op jit(solution)/shard_map/dot_general | solution.py:50
  187.9 20.3 %fusion.11 = f32[2,128,1024]{2,1,0:T(8,128)S(1)} fusion(f32[2,128,1024]{2,1,0:T(8,128)S(1)} %collective-permute-done.1), kind=kOutput, calls=%fused_computation.15 | convolution fusion | flops 3235905536 | bytes 2097152 | tf_op jit(solution)/shard_map/dot_general | solution.py:53
  208.2 20.0 %fusion.29 = f32[2,128,1024]{2,1,0:T(8,128)S(1)} fusion(f32[2,128,1024]{2,1,0:T(8,128)S(1)} %collective-permute-done.1), kind=kOutput, calls=%fused_computation.33 | convolution fusion | flops 3235905536 | bytes 2097152 | tf_op jit(solution)/shard_map/dot_general | solution.py:50
  230.2 4.7 multiply_subtract_fusion.2
  234.9 19.1 %fusion.27 = f32[2,128,1024]{2,1,0:T(8,128)S(1)} fusion(f32[1,128,1024]{1,2,0:T(8,128)S(1)} %get-tuple-element.52, f32[1,128,1024]{1,2,0:T(8,128)S(1)} %get-tuple-element.53, f32[1,128,1024]{1,2,0:T(8,128)S(1)} %get-tuple-element.28, f32[1,128,1024]{1,2,0:T(8,128)S(1)} %get-tuple-element.27), kind=kOutput, calls=%fused_computation.31 | convolution fusion | flops 3236691968 | bytes 3145728 | tf_op jit(solution)/shard_map/dot_general | solution.py:61
  254.1 19.7 %fusion.9 = f32[2,128,1024]{2,1,0:T(8,128)S(1)} fusion(f32[1,128,1024]{1,2,0:T(8,128)S(1)} %get-tuple-element.52, f32[1,128,1024]{1,2,0:T(8,128)S(1)} %get-tuple-element.53, f32[1,128,1024]{1,2,0:T(8,128)S(1)} %get-tuple-element.28, f32[1,128,1024]{1,2,0:T(8,128)S(1)} %get-tuple-element.27), kind=kOutput, calls=%fused_computation.13 | convolution fusion | flops 3236691968 | bytes 3145728 | tf_op jit(solution)/shard_map/dot_general | solution.py:64
  274.1 20.0 %fusion.25 = f32[2,128,1024]{2,1,0:T(8,128)S(1)} fusion(f32[2,128,1024]{2,1,0:T(8,128)S(1)} %maximum_multiply_fusion.1), kind=kOutput, calls=%fused_computation.29 | convolution fusion | flops 3235905536 | bytes 2097152 | tf_op jit(solution)/shard_map/dot_general | solution.py:50
  295.4 20.3 %fusion.7 = f32[2,128,1024]{2,1,0:T(8,128)S(1)} fusion(f32[2,128,1024]{2,1,0:T(8,128)S(1)} %maximum_multiply_fusion.1), kind=kOutput, calls=%fused_computation.11 | convolution fusion | flops 3235905536 | bytes 2097152 | tf_op jit(solution)/shard_map/dot_general | solution.py:53
  317.9 20.2 %fusion.23 = f32[2,128,1024]{2,1,0:T(8,128)S(1)} fusion(f32[2,128,1024]{2,1,0:T(8,128)S(1)} %collective-permute-done.2), kind=kOutput, calls=%fused_computation.27 | convolution fusion | flops 3235905536 | bytes 2097152 | tf_op jit(solution)/shard_map/dot_general | solution.py:50
  338.2 20.1 %fusion.5 = f32[2,128,1024]{2,1,0:T(8,128)S(1)} fusion(f32[2,128,1024]{2,1,0:T(8,128)S(1)} %collective-permute-done.2), kind=kOutput, calls=%fused_computation.9 | convolution fusion | flops 3235905536 | bytes 2097152 | tf_op jit(solution)/shard_map/dot_general | solution.py:53
  360.3 4.7 multiply_subtract_fusion
  365.0 19.1 %fusion.21 = f32[2,128,1024]{2,1,0:T(8,128)S(1)} fusion(f32[1,128,1024]{1,2,0:T(8,128)S(1)} %get-tuple-element.50, f32[1,128,1024]{1,2,0:T(8,128)S(1)} %get-tuple-element.51, f32[1,128,1024]{1,2,0:T(8,128)S(1)} %get-tuple-element.24, f32[1,128,1024]{1,2,0:T(8,128)S(1)} %get-tuple-element.23), kind=kOutput, calls=%fused_computation.25 | convolution fusion | flops 3236691968 | bytes 3145728 | tf_op jit(solution)/shard_map/dot_general | solution.py:61
  384.1 19.7 %fusion.3 = f32[2,128,1024]{2,1,0:T(8,128)S(1)} fusion(f32[1,128,1024]{1,2,0:T(8,128)S(1)} %get-tuple-element.50, f32[1,128,1024]{1,2,0:T(8,128)S(1)} %get-tuple-element.51, f32[1,128,1024]{1,2,0:T(8,128)S(1)} %get-tuple-element.24, f32[1,128,1024]{1,2,0:T(8,128)S(1)} %get-tuple-element.23), kind=kOutput, calls=%fused_computation.7 | convolution fusion | flops 3236691968 | bytes 3145728 | tf_op jit(solution)/shard_map/dot_general | solution.py:64
  410.9 9.0 %all-to-all-start = ((f32[16,1,32768]{2,1,0:T(1,128)}), f32[16,1,32768]{2,1,0:T(1,128)S(1)}, u32[]{:S(2)}, u32[]{:S(2)}) async-start(f32[16,1,32768]{2,1,0:T(1,128)} %copy.78), calls=%async_computation | async-start | bytes 4194304 | tf_op jit(solution)/shard_map/all_to_all | solution.py:146
  422.9 23.6 %all-to-all-done = f32[16,1,32768]{2,1,0:T(1,128)S(1)} async-done(((f32[16,1,32768]{2,1,0:T(1,128)}), f32[16,1,32768]{2,1,0:T(1,128)S(1)}, u32[]{:S(2)}, u32[]{:S(2)}) %all-to-all-start) | async-done | bytes 2097184 | tf_op jit(solution)/shard_map/all_to_all | solution.py:146
  447.9 5.0 collective-permute-start.3
  470.6 53.4 %fusion.131 = f32[2,128,128]{2,1,0:T(8,128)} fusion(f32[2,4,128]{2,1,0:T(4,128)S(1)} %collective-permute-done.4, f32[2,136,132]{2,1,0:T(8,128)S(1)} %get-tuple-element.36, f32[2,128,128]{2,1,0:T(8,128)S(1)} %bitcast.246, f32[2,136,132]{2,1,0:T(8,128)S(1)} %get-tuple-element.35, f32[2,4,128]{2,1,0:T(4,128)S(1)} %collective-permute-done.3, f32[]{:T(128)} %bitcast.135, ...), kind=kLoop, calls=%fused_computation.174 | loop fusion | flops 5537792 | bytes 9707844 | tf_op jit(solution)/shard_map/add | solution.py:158
  (71 shorter events, 52.4 us)
Async XLA Ops:
  0.0 404.4 %copy-start = (f32[1,1,8,128,128]{4,3,2,1,0:T(8,128)S(1)}, f32[1,1,8,128,128]{4,3,2,1,0:T(8,128)}, u32[]{:S(2)}) copy-start(f32[1,1,8,128,128]{4,3,2,1,0:T(8,128)} %param.15) | copy-start | bytes 1572868
  0.0 50.0 %collective-permute-start = (f32[2,128,1024]{2,1,0:T(8,128)}, f32[2,128,1024]{2,1,0:T(8,128)}, u32[]{:S(2)}, u32[]{:S(2)}) collective-permute-start(f32[2,128,1024]{2,1,0:T(8,128)} %param.9), channel_id=1, source_target_pairs={{0,8},{8,0},{16,24},{24,16},{32,40},{40,32},{48,56},{56,48},{64,72... | collective-permute-start | bytes 3145736 | tf_op jit(solution)/shard_map/ppermute | solution.py:22
  0.7 23.3 %copy-start.1 = (s32[3,1,2,8,128]{4,3,2,1,0:T(8,128)S(1)}, s32[3,1,2,8,128]{4,3,2,1,0:T(8,128)}, u32[]{:S(2)}) copy-start(s32[3,1,2,8,128]{4,3,2,1,0:T(8,128)} %param.10) | copy-start | bytes 73732
  0.7 23.3 %copy-start.2 = (f32[3,1,2,8,128]{4,3,2,1,0:T(8,128)S(1)}, f32[3,1,2,8,128]{4,3,2,1,0:T(8,128)}, u32[]{:S(2)}) copy-start(f32[3,1,2,8,128]{4,3,2,1,0:T(8,128)} %param.11) | copy-start | bytes 73732
  0.7 23.3 %copy-start.3 = (f32[3,1024]{1,0:T(4,128)S(1)}, f32[3,1024]{1,0:T(4,128)}, u32[]{:S(2)}) copy-start(f32[3,1024]{1,0:T(4,128)} %param.13) | copy-start | bytes 36868
  0.7 24.1 %copy-start.5 = (f32[3,1,2,128]{3,2,1,0:T(2,128)S(1)}, f32[3,1,2,128]{3,2,1,0:T(2,128)}, u32[]{:S(2)}) copy-start(f32[3,1,2,128]{3,2,1,0:T(2,128)} %param.12) | copy-start | bytes 9220
  0.7 25.5 %copy-start.7 = (f32[2,128,1024]{2,1,0:T(8,128)S(1)}, f32[2,128,1024]{2,1,0:T(8,128)}, u32[]{:S(2)}) copy-start(f32[2,128,1024]{2,1,0:T(8,128)} %param.9) | copy-start | bytes 3145732
  161.6 26.3 %collective-permute-start.1 = (f32[2,128,1024]{2,1,0:T(8,128)S(1)}, f32[2,128,1024]{2,1,0:T(8,128)S(1)}, u32[]{:S(2)}, u32[]{:S(2)}) collective-permute-start(f32[2,128,1024]{2,1,0:T(8,128)S(1)} %maximum_multiply_fusion), channel_id=1, source_target_pairs={{0,16},{8,24},{16,0},{24,8},{32,48},{40,56},{48,32},{56,40},{64,80... | collective-permute-start | bytes 3145736 | tf_op jit(solution)/shard_map/ppermute | solution.py:22
  294.1 23.9 %collective-permute-start.2 = (f32[2,128,1024]{2,1,0:T(8,128)S(1)}, f32[2,128,1024]{2,1,0:T(8,128)S(1)}, u32[]{:S(2)}, u32[]{:S(2)}) collective-permute-start(f32[2,128,1024]{2,1,0:T(8,128)S(1)} %maximum_multiply_fusion.1), channel_id=1, source_target_pairs={{0,32},{8,40},{16,48},{24,56},{32,0},{40,8},{48,16},{56,24},{64,96... | collective-permute-start | bytes 3145736 | tf_op jit(solution)/shard_map/ppermute | solution.py:22
  404.5 1.5 copy-start.6
  410.9 9.6 %copy-start.4 = (f32[16,81]{1,0:T(8,128)S(1)}, f32[16,81]{1,0:T(8,128)}, u32[]{:S(2)}) copy-start(f32[16,81]{1,0:T(8,128)} %param.17) | copy-start | bytes 15556
  410.9 35.6 %all-to-all-start = ((f32[16,1,32768]{2,1,0:T(1,128)}), f32[16,1,32768]{2,1,0:T(1,128)S(1)}, u32[]{:S(2)}, u32[]{:S(2)}) async-start(f32[16,1,32768]{2,1,0:T(1,128)} %copy.78), calls=%async_computation | async-start | bytes 4194304 | tf_op jit(solution)/shard_map/all_to_all | solution.py:146
  447.9 7.6 %collective-permute-start.3 = (f32[2,4,128]{2,1,0:T(4,128)S(1)}, f32[2,4,128]{2,1,0:T(4,128)S(1)}, u32[]{:S(2)}, u32[]{:S(2)}) collective-permute-start(f32[2,4,128]{2,1,0:T(4,128)S(1)} %get-tuple-element.39), channel_id=1, source_target_pairs={{0,8},{8,16},{16,24},{24,32},{32,40},{40,48},{48,56},{56,64},{64,7... | collective-permute-start | bytes 12296 | tf_op jit(solution)/shard_map/ppermute | solution.py:33
  452.9 7.3 %collective-permute-start.4 = (f32[2,4,128]{2,1,0:T(4,128)S(1)}, f32[2,4,128]{2,1,0:T(4,128)S(1)}, u32[]{:S(2)}, u32[]{:S(2)}) collective-permute-start(f32[2,4,128]{2,1,0:T(4,128)S(1)} %get-tuple-element.40), channel_id=1, source_target_pairs={{8,0},{16,8},{24,16},{32,24},{40,32},{48,40},{56,48},{64,56},{72,6... | collective-permute-start | bytes 12296 | tf_op jit(solution)/shard_map/ppermute | solution.py:35
  460.3 7.1 %collective-permute-start.5 = (f32[2,136,4]{2,1,0:T(8,128)S(1)}, f32[2,136,4]{2,1,0:T(8,128)S(1)}, u32[]{:S(2)}, u32[]{:S(2)}) collective-permute-start(f32[2,136,4]{2,1,0:T(8,128)S(1)} %get-tuple-element.37), channel_id=1, source_target_pairs={{0,1},{1,2},{2,3},{3,4},{4,5},{5,6},{6,7},{8,9},{9,10},{10,11},{11... | collective-permute-start | bytes 13064 | tf_op jit(solution)/shard_map/ppermute | solution.py:33
  462.9 7.6 %collective-permute-start.6 = (f32[2,136,4]{2,1,0:T(8,128)S(1)}, f32[2,136,4]{2,1,0:T(8,128)S(1)}, u32[]{:S(2)}, u32[]{:S(2)}) collective-permute-start(f32[2,136,4]{2,1,0:T(8,128)S(1)} %get-tuple-element.38), channel_id=1, source_target_pairs={{1,0},{2,1},{3,2},{4,3},{5,4},{6,5},{7,6},{9,8},{10,9},{11,10},{12... | collective-permute-start | bytes 13064 | tf_op jit(solution)/shard_map/ppermute | solution.py:35
where the time goes:
time: 534 us; the launch traced here: 524 us
  matrix products  382 us (72%)
  other arithmetic  72.8 us (14%)
  waiting for transfers between devices  35.5 us (7%)
  starting transfers between devices  24.6 us (5%)
  local copies, waits for them, and re-layouts  7.95 us (1%)
    dot_general x6, matrix products, forward(): jnp.dot(signal, sin_table, precision=HIGHEST_PRECISION, preferred_element...  127 us
    dot_general x6, matrix products, forward(): jnp.dot(signal, cos_table, precision=HIGHEST_PRECISION, preferred_element...  127 us
    dot_general x3, matrix products, inverse(): jnp.dot(signal, sin_table, precision=HIGHEST_PRECISION, preferred_element...  59 us
    dot_general x3, matrix products, inverse(): jnp.dot(signal, cos_table, precision=HIGHEST_PRECISION, preferred_element...  57.3 us
    add x1, other arithmetic, shards(): result_sum + kernel_row[offset] * padded[:, row_shift:row_shift + TILE_RO...  53.4 us
    all_to_all x1, waiting for transfers between devices, shards(): lax.all_to_all(outgoing, 'aper', split_axis=0, concat_axis=0, tiled=True)  23.6 us
    sub x3, other arithmetic, steer(): cos_phase * mixed[0] - sin_phase * mixed[1]  14.1 us
  transfers between devices with their start and end apart: 8, of which 6 were waited for; matrix products, arithmetic and copies ran while one was open for 19% of the time, Pallas kernels for 0%

commit v1 on v0

v1 whole, which is shorter than its diff:
```python
import functools
import math

import jax
import jax.numpy as jnp
import numpy as np
from jax import lax
from jax.experimental import pallas as pl
from jax.experimental.pallas import tpu as pltpu
from jax.sharding import PartitionSpec as P

N = 1024
H = 256
A = 128
F32 = jnp.float32
BF16 = jnp.bfloat16
VMEM = pl.BlockSpec(memory_space=pltpu.VMEM)
SMEM = pl.BlockSpec(memory_space=pltpu.SMEM)


def dft_tables():
    r = np.arange(H)[:, None]
    out = []
    for m1 in range(4):
        m = 4 * np.arange(H)[None, :] + m1
        angle = 2.0 * np.pi * ((r * m) % N) / N
        c, s = np.cos(angle), np.sin(angle)
        out.append(np.stack([np.concatenate([c, s], 1), np.concatenate([c.T, s.T], 1)]))
    full = np.stack(out, 1).astype(np.float32)
    hi = full.astype(jnp.bfloat16)
    lo = (full - hi.astype(np.float32)).astype(jnp.bfloat16)
    return hi, lo


def split(x):
    hi = x.astype(BF16)
    return hi, (x - hi.astype(F32)).astype(BF16)


def dot(a, b):
    return jnp.dot(a, b, preferred_element_type=F32)


def quarter_turns(re, im, sign):
    ar, ai = re[0] + re[2], im[0] + im[2]
    br, bi = re[0] - re[2], im[0] - im[2]
    cr, ci = re[1] + re[3], im[1] + im[3]
    dr, di = re[1] - re[3], im[1] - im[3]
    if sign > 0:
        er, ei = -di, dr
    else:
        er, ei = di, -dr
    return [ar + cr, br + er, ar - cr, br - er], [ai + ci, bi + ei, ai - ci, bi - ei]


def sincos_turns(t):
    t = t - jnp.round(t)
    q = jnp.round(t * 4.0)
    y = (t - q * 0.25) * F32(2.0 * math.pi)
    y2 = y * y
    s = y * (1.0 + y2 * (-1.0 / 6 + y2 * (1.0 / 120 + y2 * (-1.0 / 5040 + y2 * (1.0 / 362880)))))
    c = 1.0 + y2 * (-0.5 + y2 * (1.0 / 24 + y2 * (-1.0 / 720 + y2 * (1.0 / 40320 - y2 * (1.0 / 3628800)))))
    odd = jnp.abs(q) == 1.0
    half = jnp.abs(q) == 2.0
    sign = jnp.where(q < 0, -1.0, 1.0)
    cc = jnp.where(odd, -sign * s, jnp.where(half, -c, c))
    ss = jnp.where(odd, sign * c, jnp.where(half, -s, s))
    return cc, ss


def prepare(tab, at, mats, phases, steps):
    rows = lax.broadcasted_iota(jnp.int32, (A, A), 0).astype(F32)
    total = jnp.zeros((A, A), F32)
    for t in range(8):
        total = total + jnp.where(rows == tab[t : t + 1, :], tab[8 + t : 9 + t, :], 0.0)
    hi, lo = split(total.T)
    mats[at, 0:A, 0:A] = hi
    mats[at, 0:A, A:] = hi
    mats[at, A:, 0:A] = lo
    mats[at, A:, A:] = jnp.zeros((A, A), BF16)
    shift = jnp.broadcast_to(tab[16:17, :], (A, A)).T
    lane = lax.broadcasted_iota(jnp.int32, (A, A), 1).astype(F32)
    c, s = sincos_turns(shift * lane * F32(-4.0 / N))
    hc, hs = sincos_turns(shift * F32(0.5))
    phases[at, 0, :, 0:A] = c
    phases[at, 1, :, 0:A] = s
    phases[at, 0, :, A:] = c * hc - s * hs
    phases[at, 1, :, A:] = c * hs + s * hc
    c1, s1 = sincos_turns(shift * F32(-1.0 / N))
    steps[at, 0] = c1
    steps[at, 1] = s1


def put_split(ref, m1, signals, n, which, re, im):
    rh, rl = split(re)
    ih, il = split(im)
    for part, value in enumerate((rh, ih, rl, il)):
        base = (part // 2) * 2 * n * A + (part % 2) * n * A + which * A
        ref[m1, base : base + A, :] = value


def product(lhs, hi, lo, rows):
    both = dot(lhs, hi)
    return both[:rows] + both[rows:] + dot(lhs[:rows], lo)


def stage(inputs, plan, zz, uu, hi_ref, lo_ref, mats, phases, steps):
    n_in, n_out = len(inputs), len(plan)
    for which, (re, im) in enumerate(inputs):
        zr, zi = quarter_turns(re, im, -1)
        for m1 in range(4):
            put_split(zz, m1, None, n_in, which, zr[m1], zi[m1])

    def body(m1, carry):
        rows = 2 * n_in * A
        p = product(zz[m1, : 2 * rows, :], hi_ref[0, m1], lo_ref[0, m1], rows)
        half = n_in * A
        xr = p[:half, :H] + p[half:, H:]
        xi = p[half:, :H] - p[:half, H:]
        stacked = []
        for which in range(n_in):
            x = jnp.concatenate([xr[which * A : which * A + A], xi[which * A : which * A + A]], axis=1)
            h, l = split(x)
            stacked.append(jnp.concatenate([h, l], axis=0))
        parts = [[], [], [], []]
        for terms in plan:
            mr = mi = None
            for which, at in terms:
                y = dot(mats[at], stacked[which])
                y = y[:A] + y[A:]
                yr, yi = y[:, :H], y[:, H:]
                c, s = phases[at, 0], phases[at, 1]
                tr, ti = c * yr - s * yi, c * yi + s * yr
                mr, mi = (tr, ti) if mr is None else (mr + tr, mi + ti)
                c1, s1 = steps[at, 0], steps[at, 1]
                c1 = jnp.concatenate([c1, c1], axis=1)
                s1 = jnp.concatenate([s1, s1], axis=1)
                phases[at, 0] = c * c1 - s * s1
                phases[at, 1] = c * s1 + s * c1
            rh, rl = split(mr)
            ih, il = split(mi)
            for k, v in enumerate((rh, ih, rl, il)):
                parts[k].append(v)
        lhs = jnp.concatenate([v for part in parts for v in part], axis=0)
        rows = 2 * n_out * A
        p = product(lhs, hi_ref[1, m1], lo_ref[1, m1], rows)
        half = n_out * A
        uu[m1, :half, :H] = p[:half, :H] - p[half:, H:]
        uu[m1, :half, H:] = p[:half, H:] + p[half:, :H]
        return carry

    lax.fori_loop(0, 4, body, 0)
    out = []
    for which in range(n_out):
        base = which * A
        re = [uu[m1, base : base + A, :H] for m1 in range(4)]
        im = [uu[m1, base : base + A, H:] for m1 in range(4)]
        out.append(quarter_turns(re, im, 1))
    return out


def gained(blocks, gain, section):
    re, im = blocks
    rows = [gain[section : section + 1, H * k : H * k + H] * F32(1.0 / N) for k in range(4)]
    return [v * g for v, g in zip(re, rows)], [v * g for v, g in zip(im, rows)]


def merge_kernel(bits, own, other, tab, tabx, taby, tabd, gain, hi, lo, out, zz, uu, mats, phases, steps):
    b0, b1, b2 = bits[0], bits[1], bits[2]
    prepare(tab[b0], 0, mats, phases, steps)
    prepare(tab[1 - b0], 1, mats, phases, steps)
    prepare(tab[2 + b1], 2, mats, phases, steps)
    prepare(tabx[2 + b1], 3, mats, phases, steps)
    for at, ref in ((4, tab), (5, tabx), (6, taby), (7, tabd)):
        prepare(ref[4 + b2], at, mats, phases, steps)
    run = functools.partial(stage, zz=zz, uu=uu, hi_ref=hi, lo_ref=lo, mats=mats, phases=phases, steps=steps)

    def blocks(ref):
        return [[ref[p, :, H * k : H * k + H] for k in range(4)] for p in range(2)]

    first = run([blocks(own), blocks(other)], [[(0, 0), (1, 1)]])
    y = gained(first[0], gain, 0)
    second = run([y], [[(0, 2)], [(0, 3)]])
    z = [gained(v, gain, 1) for v in second]
    third = run(z, [[(0, 4)], [(1, 5)], [(0, 6)], [(1, 7)]])
    for j, v in enumerate(third):
        re, im = gained(v, gain, 2)
        for k in range(4):
            for part in range(2):
                both = jnp.concatenate(
                    [re[k][:, A * part : A * part + A], im[k][:, A * part : A * part + A]], axis=1
                )
                h, l = split(both)
                out[j, 2 * k + part, 0:A] = h
                out[j, 2 * k + part, A:] = l


ROWS = A + 8


def contrib_kernel(owners, bits, cur, w0, w1, w2, w3, keep, send, acc):
    acc[...] = jnp.zeros_like(acc)
    row = lax.broadcasted_iota(jnp.int32, (8, H), 0)

    def place(owner):
        return (owner % 2) * 8 + owner // 2

    for j, w in enumerate((w0, w1, w2, w3)):

        def body(q, carry):
            h, l = split(w[q])
            x = cur[j, q]
            c = dot(h, x[:A]) + dot(l, x[:A]) + dot(h, x[A:])
            owner = owners[j * 8 + q]
            acc[place(owner), 0:A] += c
            top = pltpu.roll(c[A - 8 :], 4, 0)
            bottom = pltpu.roll(c[:8], 4, 0)

            @pl.when(owner < 15)
            def _():
                acc[place(owner + 1), A:] += jnp.where(row < 4, top, 0.0)

            @pl.when(owner > 0)
            def _():
                acc[place(owner - 1), A:] += jnp.where(row >= 4, bottom, 0.0)

            return carry

        lax.fori_loop(0, 8, body, 0)
    mine = pl.multiple_of(bits[0] * 8, 8)
    theirs = pl.multiple_of(8 - bits[0] * 8, 8)
    keep[...] = acc[pl.ds(mine, 8)]
    send[...] = acc[pl.ds(theirs, 8)]


def add_kernel(a, b, out):
    out[...] = a[...] + b[...]


def tile_kernel(parts, tile, first, last):
    total = parts[0]
    for k in range(1, 8):
        total = total + parts[k]
    tile[...] = total
    first[...] = jnp.concatenate([total[:, 0:A], total[:, A:]], axis=0)
    last[...] = jnp.concatenate([total[:, 0:A], total[:, A:]], axis=0)


def filter_kernel(index, bank, tile, before, after, out, pad, moved):
    number = index[0, 0]
    for p in range(2):
        body = tile[:, A * p : A * p + A]
        lead = before[ROWS * p : ROWS * p + ROWS, :]
        tail = after[ROWS * p : ROWS * p + ROWS, :]
        lane = lax.broadcasted_iota(jnp.int32, (ROWS, A), 1)
        turned = pltpu.roll(body, 4, 1)
        left = jnp.where(lane < 4, pltpu.roll(lead, 4, 1), turned)
        right = jnp.where(lane < 4, turned, pltpu.roll(tail, 4, 1))
        for half, value in enumerate((left, right)):
            pad[4 : 4 + A, A * half : A * half + A] = value[0:A]
            pad[0:4, A * half : A * half + A] = value[A : A + 4]
            pad[A + 4 :, A * half : A * half + A] = value[A + 4 :]
        total = jnp.zeros((A, A), F32)
        for v in range(9):
            if v:
                moved[...] = pltpu.roll(pad[...], H - v, 1)[:, :A]
            else:
                moved[...] = pad[:, :A]
            for u in range(9):
                total = total + bank[number, 9 * u + v] * moved[u : u + A, :]
        out[p] = total


def call(kernel, out_shape, in_specs, scratch=(), flops=1000000):
    return pl.pallas_call(
        kernel,
        out_shape=out_shape,
        in_specs=in_specs,
        out_specs=jax.tree.map(lambda _: VMEM, out_shape),
        scratch_shapes=list(scratch),
        compiler_params=pltpu.CompilerParams(vmem_limit_bytes=48 << 20),
        cost_estimate=pl.CostEstimate(flops=flops, bytes_accessed=1 << 20, transcendentals=0),
    )


def struct(shape, dtype=F32):
    return jax.ShapeDtypeStruct(shape, dtype)


def swap(value, mask):
    return lax.ppermute(value, "aper", [(i, i ^ mask) for i in range(16)])


def shards(polar, tap_index, tap_weight, range_shift, range_gain, tile_owner, weights, kernel_index, bank):
    place = lax.axis_index("aper")
    bits = jnp.stack([place % 2, place // 2 % 2, place // 4 % 2]).astype(jnp.int32)
    owner_row = jnp.zeros((8, A), F32).at[:, 0:8].set(tile_owner[0, 0, :, 0].astype(F32)[None, :])
    tab = jnp.concatenate(
        [
            tap_index[:, 0].astype(F32),
            tap_weight[:, 0],
            jnp.broadcast_to(range_shift[:, 0, :, None, :], (3, 2, 4, A)),
            jnp.broadcast_to(owner_row[0:4], (3, 2, 4, A)),
        ],
        axis=2,
    ).reshape(6, 24, A)
    tabx, taby, tabd = (swap(tab, mask) for mask in (2, 4, 6))
    other = swap(polar, 1)
    own_weights = weights[0, 0]
    wx, wy, wd = (swap(own_weights, mask) for mask in (2, 4, 6))
    hi, lo = dft_tables()
    cur = call(
        merge_kernel,
        struct((4, 8, 2 * A, H), BF16),
        [SMEM] + [VMEM] * 9,
        [
            pltpu.VMEM((4, 8 * A, H), BF16),
            pltpu.VMEM((4, 4 * A, 2 * H), F32),
            pltpu.VMEM((8, 2 * A, 2 * A), BF16),
            pltpu.VMEM((8, 2, A, H), F32),
            pltpu.VMEM((8, 2, A, A), F32),
        ],
        flops=12 * 10**9,
    )(bits, polar, other, tab, tabx, taby, tabd, range_gain, jnp.asarray(hi), jnp.asarray(lo))
    owners = jnp.concatenate([t[0, 20, 0:8] for t in (tab, tabx, taby, tabd)]).astype(jnp.int32)
    keep, send = call(
        contrib_kernel,
        (struct((8, ROWS, H)), struct((8, ROWS, H))),
        [SMEM, SMEM] + [VMEM] * 5,
        [pltpu.VMEM((16, ROWS, H), F32)],
        flops=10**9,
    )(owners, bits, cur, own_weights, wx, wy, wd)
    taken = swap(send, 1)
    half = keep + taken
    groups = [[c + 2 * k for k in range(8)] for c in range(2)]
    parts = lax.all_to_all(half, "aper", split_axis=0, concat_axis=0, axis_index_groups=groups, tiled=True)
    tile, first, last = call(
        tile_kernel, (struct((ROWS, H)), struct((2 * ROWS, A)), struct((2 * ROWS, A))), [VMEM]
    )(parts)
    before = lax.ppermute(last, "swath", [(i, i + 1) for i in range(7)])
    after = lax.ppermute(first, "swath", [(i + 1, i) for i in range(7)])
    return call(
        filter_kernel,
        struct((2, A, A)),
        [SMEM, SMEM] + [VMEM] * 3,
        [pltpu.VMEM((ROWS, H), F32), pltpu.VMEM((ROWS, A), F32)],
    )(kernel_index, bank, tile, before, after)


def solution(mesh):
    in_specs = (
        P(None, "aper", "swath"),
        P(None, "aper", None, None, None),
        P(None, "aper", None, None, None),
        P(None, "aper", None, None),
        P(None, "swath"),
        P("aper", "swath", None, None),
        P("aper", "swath", None, None, None),
        P("aper", "swath"),
        P(),
    )
    out_specs = P(None, "aper", "swath")
    return jax.shard_map(shards, mesh=mesh, in_specs=in_specs, out_specs=out_specs, check_vma=False)
```

time: 534 us -> 107 us (0.20)
  the two profiles are of different devices: /device:TPU:39 before, /device:TPU:34 now
where the time goes in v1:
time: 107 us; the launch traced here: 106 us
  Pallas kernels  45 us (42%)
  blocking collectives  24.4 us (23%)
  starting transfers between devices  16.6 us (16%)
  waiting for transfers between devices  11.8 us (11%)
  local copies, waits for them, and re-layouts  4.31 us (4%)
  other arithmetic  3.74 us (3%)
    pallas_call x1, Pallas kernels, shards(): call(merge_kernel, struct((4, 8, 2 * A, H), BF16), [SMEM] + [VMEM] * 9, [...  32.8 us
    all_to_all x1, blocking collectives, shards(): lax.all_to_all(half, 'aper', split_axis=0, concat_axis=0, axis_index_grou...  24.4 us
    ppermute x8, starting transfers between devices, swap(): return lax.ppermute(value, 'aper', [(i, i ^ mask) for i in range(16)])  9.67 us
    pallas_call x1, Pallas kernels, shards(): call(contrib_kernel, (struct((8, ROWS, H)), struct((8, ROWS, H))), [SMEM,...  9.52 us
    ppermute x8, waiting for transfers between devices, swap(): return lax.ppermute(value, 'aper', [(i, i ^ mask) for i in range(16)])  6.5 us
    ppermute x1, starting transfers between devices, shards(): before = lax.ppermute(last, 'swath', [(i, i + 1) for i in range(7)])  5 us
    ppermute x1, waiting for transfers between devices, shards(): after = lax.ppermute(first, 'swath', [(i + 1, i) for i in range(7)])  3.98 us
    unnamed x10, local copies, waits for them, and re-layouts  3.6 us
  transfers between devices with their start and end apart: 10, of which 4 were waited for; matrix products, arithmetic and copies ran while one was open for 4% of the time, Pallas kernels for 31%

profile of v1, /device:TPU:34, one launch (start us, length us, event | category | flops | bytes accessed | tf_op | source)
XLA Modules:
  0.0 106.5 jit_solution(10123674093753228973)
XLA Ops:
  0.0 0.6 compare_reduce_fusion
  0.6 1.3 %fusion = f32[8]{0:T(128)S(1)} fusion(pred[]{:T(512)} %compare_reduce_fusion, s32[1,1,8,1]{2,3,1,0:T(1,128)} %param.18), kind=kLoop, calls=%fused_computation.3 | loop fusion | flops 16 | bytes 65 | tf_op jit(solution)/shard_map/squeeze | solution.py:325
  1.9 0.7 convert_element_type.19
  2.7 0.7 broadcast_in_dim.6
  3.4 0.8 pad_maximum_fusion.tab
  4.2 2.2 %collective-permute-start = (f32[6,24,128]{2,1,0:T(8,128)S(1)}, f32[6,24,128]{2,1,0:T(8,128)S(1)}, u32[]{:S(2)}, u32[]{:S(2)}) collective-permute-start(f32[6,24,128]{2,1,0:T(8,128)S(1)} %pad_maximum_fusion.tab), channel_id=1, source_target_pairs={{0,16},{8,24},{16,0},{24,8},{32,48},{40,56},{48,32},{56,40},{64,80... | collective-permute-start | bytes 221192 | tf_op jit(solution)/shard_map/ppermute | solution.py:291
  6.4 1.6 %collective-permute-start.1 = (f32[6,24,128]{2,1,0:T(8,128)S(1)}, f32[6,24,128]{2,1,0:T(8,128)S(1)}, u32[]{:S(2)}, u32[]{:S(2)}) collective-permute-start(f32[6,24,128]{2,1,0:T(8,128)S(1)} %pad_maximum_fusion.tab), channel_id=1, source_target_pairs={{0,32},{8,40},{16,48},{24,56},{32,0},{40,8},{48,16},{56,24},{64,96... | collective-permute-start | bytes 221192 | tf_op jit(solution)/shard_map/ppermute | solution.py:291
  7.9 1.3 %collective-permute-start.2 = (f32[6,24,128]{2,1,0:T(8,128)S(1)}, f32[6,24,128]{2,1,0:T(8,128)S(1)}, u32[]{:S(2)}, u32[]{:S(2)}) collective-permute-start(f32[6,24,128]{2,1,0:T(8,128)S(1)} %pad_maximum_fusion.tab), channel_id=1, source_target_pairs={{0,48},{8,56},{16,32},{24,40},{32,16},{40,24},{48,0},{56,8},{64,11... | collective-permute-start | bytes 221192 | tf_op jit(solution)/shard_map/ppermute | solution.py:291
  9.2 2.1 %collective-permute-start.4 = (f32[8,128,128]{2,1,0:T(8,128)}, f32[8,128,128]{2,1,0:T(8,128)S(1)}, u32[]{:S(2)}, u32[]{:S(2)}) collective-permute-start(f32[8,128,128]{2,1,0:T(8,128)} %bitcast.14), channel_id=1, source_target_pairs={{0,16},{8,24},{16,0},{24,8},{32,48},{40,56},{48,32},{56,40},{64,80... | collective-permute-start | bytes 1572872 | tf_op jit(solution)/shard_map/ppermute | solution.py:291
  11.4 3.7 %collective-permute-done.2.tabd = f32[6,24,128]{2,1,0:T(8,128)S(1)} collective-permute-done((f32[6,24,128]{2,1,0:T(8,128)S(1)}, f32[6,24,128]{2,1,0:T(8,128)S(1)}, u32[]{:S(2)}, u32[]{:S(2)}) %collective-permute-start.2) | collective-permute-done | bytes 73760 | tf_op jit(solution)/shard_map/ppermute | solution.py:291
  15.2 0.4 collective-permute-start.5
  15.6 1.9 %collective-permute-start.6 = (f32[8,128,128]{2,1,0:T(8,128)}, f32[8,128,128]{2,1,0:T(8,128)S(1)}, u32[]{:S(2)}, u32[]{:S(2)}) collective-permute-start(f32[8,128,128]{2,1,0:T(8,128)} %bitcast.16), channel_id=1, source_target_pairs={{0,48},{8,56},{16,32},{24,40},{32,16},{40,24},{48,0},{56,8},{64,11... | collective-permute-start | bytes 1572872 | tf_op jit(solution)/shard_map/ppermute | solution.py:291
  17.7 1.3 %copy-done.2 = f32[2,128,1024]{2,1,0:T(8,128)S(1)} copy-done((f32[2,128,1024]{2,1,0:T(8,128)S(1)}, f32[2,128,1024]{2,1,0:T(8,128)}, u32[]{:S(2)}) %copy-start.2) | copy-done | bytes 1048600
  19.0 0.7 copy-done.3
  19.7 1.6 %copy-done.4 = bf16[2,4,256,512]{3,2,1,0:T(8,128)(2,1)S(1)} copy-done((bf16[2,4,256,512]{3,2,1,0:T(8,128)(2,1)S(1)}, bf16[2,4,256,512]{3,2,1,0:T(8,128)(2,1)}, u32[]{:S(2)}) %copy-start.4) | copy-done | bytes 2097176
  21.3 32.8 %shard_map.109.cur = bf16[4,8,256,256]{3,2,1,0:T(8,128)(2,1)} custom-call(s32[3]{0:T(128)S(1)} %pad_add_fusion.bits, f32[2,128,1024]{2,1,0:T(8,128)S(1)} %copy-done.2, f32[2,128,1024]{2,1,0:T(8,128)S(1)} %collective-permute-done.3.other, f32[6,24,128]{2,1,0:T(8,128)S(1)} %pad_maximum_fusion.tab, f32[6,24,128]{2,1,0:T(8,128)S(1)} %collective-permute-done.tabx, ...), custom_call_target="tpu_custom_call" | custom-call | flops 12000000000 | bytes 1048576 | tf_op jit(solution)/shard_map/pallas_call | solution.py:312
  54.1 9.5 %shard_map.110 = (f32[8,136,256]{2,1,0:T(8,128)S(1)}, f32[8,136,256]{2,1,0:T(8,128)S(1)}) custom-call(s32[32]{0:T(128)S(1)} %maximum_convert_fusion.owners, s32[3]{0:T(128)S(1)} %pad_add_fusion.bits, bf16[4,8,256,256]{3,2,1,0:T(8,128)(2,1)} %shard_map.109.cur, f32[8,128,128]{2,1,0:T(8,128)S(1)} %bitcast.17, f32[8,128,128]{2,1,0:T(8,128)S(1)} %collective-permute-done.4.w1, ...), custom_call_target="tpu_custom_call" | custom-call | flops 1000000000 | bytes 1048576 | tf_op jit(solution)/shard_map/pallas_call | solution.py:326
  63.7 2.7 %collective-permute-done.7 = f32[8,136,256]{2,1,0:T(8,128)S(1)} collective-permute-done((f32[8,136,256]{2,1,0:T(8,128)S(1)}, f32[8,136,256]{2,1,0:T(8,128)S(1)}, u32[]{:S(2)}, u32[]{:S(2)}) %collective-permute-start.7) | collective-permute-done | bytes 1114144 | tf_op jit(solution)/shard_map/ppermute | solution.py:291
  66.6 24.4 %all_to_all.5.parts = f32[8,136,256]{2,1,0:T(8,128)S(1)} all-to-all(f32[8,136,256]{2,1,0:T(8,128)S(1)} %add.22), channel_id=1, replica_groups={{0,16,32,48,64,80,96,112},{8,24,40,56,72,88,104,120},{1,17,33,49,65,81,..., dimensions={0} | all-to-all | bytes 2228224 | tf_op jit(solution)/shard_map/all_to_all | solution.py:336
  91.0 5.0 %collective-permute-start.8 = (f32[272,128]{1,0:T(8,128)S(1)}, f32[272,128]{1,0:T(8,128)S(1)}, u32[]{:S(2)}, u32[]{:S(2)}) collective-permute-start(f32[272,128]{1,0:T(8,128)S(1)} %get-tuple-element.25), channel_id=1, source_target_pairs={{0,1},{1,2},{2,3},{3,4},{4,5},{5,6},{6,7},{8,9},{9,10},{10,11},{11... | collective-permute-start | bytes 417800 | tf_op jit(solution)/shard_map/ppermute | solution.py:340
  96.1 1.9 %collective-permute-start.9 = (f32[272,128]{1,0:T(8,128)S(1)}, f32[272,128]{1,0:T(8,128)S(1)}, u32[]{:S(2)}, u32[]{:S(2)}) collective-permute-start(f32[272,128]{1,0:T(8,128)S(1)} %get-tuple-element.26), channel_id=1, source_target_pairs={{1,0},{2,1},{3,2},{4,3},{5,4},{6,5},{7,6},{9,8},{10,9},{11,10},{12... | collective-permute-start | bytes 417800 | tf_op jit(solution)/shard_map/ppermute | solution.py:341
  98.6 1.3 %collective-permute-done.8.before = f32[272,128]{1,0:T(8,128)S(1)} collective-permute-done((f32[272,128]{1,0:T(8,128)S(1)}, f32[272,128]{1,0:T(8,128)S(1)}, u32[]{:S(2)}, u32[]{:S(2)}) %collective-permute-start.8) | collective-permute-done | bytes 139296 | tf_op jit(solution)/shard_map/ppermute | solution.py:340
  99.9 4.0 %collective-permute-done.9.after = f32[272,128]{1,0:T(8,128)S(1)} collective-permute-done((f32[272,128]{1,0:T(8,128)S(1)}, f32[272,128]{1,0:T(8,128)S(1)}, u32[]{:S(2)}, u32[]{:S(2)}) %collective-permute-start.9) | collective-permute-done | bytes 139296 | tf_op jit(solution)/shard_map/ppermute | solution.py:341
  103.9 2.5 %shard_map.112 = f32[2,128,128]{2,1,0:T(8,128)} custom-call(s32[1,1]{1,0:T(1,128)S(6)} %copy.12.index, f32[16,81]{1,0:T(8,128)S(1)} %copy-done.1, f32[136,256]{1,0:T(8,128)S(1)} %get-tuple-element.24.tile, f32[272,128]{1,0:T(8,128)S(1)} %collective-permute-done.8.before, f32[272,128]{1,0:T(8,128)S(1)} %collective-permute-done.9.after), custom_call_target="tpu_custom_call" | custom-call | flops 1000000 | bytes 1048576 | tf_op jit(solution)/shard_map/pallas_call | solution.py:342
  (25 shorter events, 0.5 us)
Async XLA Ops:
  0.0 17.7 %collective-permute-start.3 = (f32[2,128,1024]{2,1,0:T(8,128)}, f32[2,128,1024]{2,1,0:T(8,128)S(1)}, u32[]{:S(2)}, u32[]{:S(2)}) collective-permute-start(f32[2,128,1024]{2,1,0:T(8,128)} %own.1), channel_id=1, source_target_pairs={{0,8},{8,0},{16,24},{24,16},{32,40},{40,32},{48,56},{56,48},{64,72... | collective-permute-start | bytes 3145736 | tf_op jit(solution)/shard_map/ppermute | solution.py:291
  4.2 13.4 %collective-permute-start = (f32[6,24,128]{2,1,0:T(8,128)S(1)}, f32[6,24,128]{2,1,0:T(8,128)S(1)}, u32[]{:S(2)}, u32[]{:S(2)}) collective-permute-start(f32[6,24,128]{2,1,0:T(8,128)S(1)} %pad_maximum_fusion.tab), channel_id=1, source_target_pairs={{0,16},{8,24},{16,0},{24,8},{32,48},{40,56},{48,32},{56,40},{64,80... | collective-permute-start | bytes 221192 | tf_op jit(solution)/shard_map/ppermute | solution.py:291
  6.4 9.3 %collective-permute-start.1 = (f32[6,24,128]{2,1,0:T(8,128)S(1)}, f32[6,24,128]{2,1,0:T(8,128)S(1)}, u32[]{:S(2)}, u32[]{:S(2)}) collective-permute-start(f32[6,24,128]{2,1,0:T(8,128)S(1)} %pad_maximum_fusion.tab), channel_id=1, source_target_pairs={{0,32},{8,40},{16,48},{24,56},{32,0},{40,8},{48,16},{56,24},{64,96... | collective-permute-start | bytes 221192 | tf_op jit(solution)/shard_map/ppermute | solution.py:291
  7.9 7.2 %collective-permute-start.2 = (f32[6,24,128]{2,1,0:T(8,128)S(1)}, f32[6,24,128]{2,1,0:T(8,128)S(1)}, u32[]{:S(2)}, u32[]{:S(2)}) collective-permute-start(f32[6,24,128]{2,1,0:T(8,128)S(1)} %pad_maximum_fusion.tab), channel_id=1, source_target_pairs={{0,48},{8,56},{16,32},{24,40},{32,16},{40,24},{48,0},{56,8},{64,11... | collective-permute-start | bytes 221192 | tf_op jit(solution)/shard_map/ppermute | solution.py:291
  9.2 44.9 %collective-permute-start.4 = (f32[8,128,128]{2,1,0:T(8,128)}, f32[8,128,128]{2,1,0:T(8,128)S(1)}, u32[]{:S(2)}, u32[]{:S(2)}) collective-permute-start(f32[8,128,128]{2,1,0:T(8,128)} %bitcast.14), channel_id=1, source_target_pairs={{0,16},{8,24},{16,0},{24,8},{32,48},{40,56},{48,32},{56,40},{64,80... | collective-permute-start | bytes 1572872 | tf_op jit(solution)/shard_map/ppermute | solution.py:291
  15.2 38.9 %collective-permute-start.5 = (f32[8,128,128]{2,1,0:T(8,128)}, f32[8,128,128]{2,1,0:T(8,128)S(1)}, u32[]{:S(2)}, u32[]{:S(2)}) collective-permute-start(f32[8,128,128]{2,1,0:T(8,128)} %bitcast.15), channel_id=1, source_target_pairs={{0,32},{8,40},{16,48},{24,56},{32,0},{40,8},{48,16},{56,24},{64,96... | collective-permute-start | bytes 1572872 | tf_op jit(solution)/shard_map/ppermute | solution.py:291
  15.6 38.5 %collective-permute-start.6 = (f32[8,128,128]{2,1,0:T(8,128)}, f32[8,128,128]{2,1,0:T(8,128)S(1)}, u32[]{:S(2)}, u32[]{:S(2)}) collective-permute-start(f32[8,128,128]{2,1,0:T(8,128)} %bitcast.16), channel_id=1, source_target_pairs={{0,48},{8,56},{16,32},{24,40},{32,16},{40,24},{48,0},{56,8},{64,11... | collective-permute-start | bytes 1572872 | tf_op jit(solution)/shard_map/ppermute | solution.py:291
  17.7 36.5 %copy-start = (f32[1,1,8,128,128]{4,3,2,1,0:T(8,128)S(1)}, f32[1,1,8,128,128]{4,3,2,1,0:T(8,128)}, u32[]{:S(2)}) copy-start(f32[1,1,8,128,128]{4,3,2,1,0:T(8,128)} %param.19) | copy-start | bytes 1572868
  17.7 1.3 %copy-start.2 = (f32[2,128,1024]{2,1,0:T(8,128)S(1)}, f32[2,128,1024]{2,1,0:T(8,128)}, u32[]{:S(2)}) copy-start(f32[2,128,1024]{2,1,0:T(8,128)} %own.1) | copy-start | bytes 3145732
  19.0 0.7 copy-start.3
  19.7 1.6 %copy-start.4 = (bf16[2,4,256,512]{3,2,1,0:T(8,128)(2,1)S(1)}, bf16[2,4,256,512]{3,2,1,0:T(8,128)(2,1)}, u32[]{:S(2)}) copy-start(bf16[2,4,256,512]{3,2,1,0:T(8,128)(2,1)} %constant.82.clone.hi) | copy-start | bytes 6291460
  63.6 2.8 %collective-permute-start.7 = (f32[8,136,256]{2,1,0:T(8,128)S(1)}, f32[8,136,256]{2,1,0:T(8,128)S(1)}, u32[]{:S(2)}, u32[]{:S(2)}) collective-permute-start(f32[8,136,256]{2,1,0:T(8,128)S(1)} %get-tuple-element.23), channel_id=1, source_target_pairs={{0,8},{8,0},{16,24},{24,16},{32,40},{40,32},{48,56},{56,48},{64,72... | collective-permute-start | bytes 3342344 | tf_op jit(solution)/shard_map/ppermute | solution.py:291
  91.0 12.9 %copy-start.1 = (f32[16,81]{1,0:T(8,128)S(1)}, f32[16,81]{1,0:T(8,128)}, u32[]{:S(2)}) copy-start(f32[16,81]{1,0:T(8,128)} %bank.1) | copy-start | bytes 15556
  91.0 8.9 %collective-permute-start.8 = (f32[272,128]{1,0:T(8,128)S(1)}, f32[272,128]{1,0:T(8,128)S(1)}, u32[]{:S(2)}, u32[]{:S(2)}) collective-permute-start(f32[272,128]{1,0:T(8,128)S(1)} %get-tuple-element.25), channel_id=1, source_target_pairs={{0,1},{1,2},{2,3},{3,4},{4,5},{5,6},{6,7},{8,9},{9,10},{10,11},{11... | collective-permute-start | bytes 417800 | tf_op jit(solution)/shard_map/ppermute | solution.py:340
  96.1 7.8 %collective-permute-start.9 = (f32[272,128]{1,0:T(8,128)S(1)}, f32[272,128]{1,0:T(8,128)S(1)}, u32[]{:S(2)}, u32[]{:S(2)}) collective-permute-start(f32[272,128]{1,0:T(8,128)S(1)} %get-tuple-element.26), channel_id=1, source_target_pairs={{1,0},{2,1},{3,2},{4,3},{5,4},{6,5},{7,6},{9,8},{10,9},{11,10},{12... | collective-permute-start | bytes 417800 | tf_op jit(solution)/shard_map/ppermute | solution.py:341

commit v2 on v1

--- a/solution.py
+++ b/solution.py
@@ -19,13 +19,14 @@
 
 
 def dft_tables():
-    r = np.arange(H)[:, None]
+    r = np.arange(A)[:, None]
     out = []
-    for m1 in range(4):
-        m = 4 * np.arange(H)[None, :] + m1
+    for m1 in range(8):
+        m = 8 * np.arange(A)[None, :] + m1
         angle = 2.0 * np.pi * ((r * m) % N) / N
         c, s = np.cos(angle), np.sin(angle)
-        out.append(np.stack([np.concatenate([c, s], 1), np.concatenate([c.T, s.T], 1)]))
+        forward = np.block([[c, -s], [s, c]])
+        out.append(np.stack([forward, forward.T]))
     full = np.stack(out, 1).astype(np.float32)
     hi = full.astype(jnp.bfloat16)
     lo = (full - hi.astype(np.float32)).astype(jnp.bfloat16)
@@ -51,6 +52,21 @@
     else:
         er, ei = di, -dr
     return [ar + cr, br + er, ar - cr, br - er], [ai + ci, bi + ei, ai - ci, bi - ei]
+
+
+def eighth_turns(re, im, sign):
+    er, ei = quarter_turns(re[0::2], im[0::2], sign)
+    br, bi = quarter_turns(re[1::2], im[1::2], sign)
+    root = F32(math.sqrt(0.5))
+    if sign > 0:
+        tr = [br[0], (br[1] - bi[1]) * root, -bi[2], (br[3] + bi[3]) * -root]
+        ti = [bi[0], (bi[1] + br[1]) * root, br[2], (br[3] - bi[3]) * root]
+    else:
+        tr = [br[0], (br[1] + bi[1]) * root, bi[2], (bi[3] - br[3]) * root]
+        ti = [bi[0], (bi[1] - br[1]) * root, -br[2], (bi[3] + br[3]) * -root]
+    out_re = [e + t for e, t in zip(er, tr)] + [e - t for e, t in zip(er, tr)]
+    out_im = [e + t for e, t in zip(ei, ti)] + [e - t for e, t in zip(ei, ti)]
+    return out_re, out_im
 
 
 def sincos_turns(t):
@@ -79,26 +95,16 @@
     mats[at, A:, 0:A] = lo
     mats[at, A:, A:] = jnp.zeros((A, A), BF16)
     shift = jnp.broadcast_to(tab[16:17, :], (A, A)).T
-    lane = lax.broadcasted_iota(jnp.int32, (A, A), 1).astype(F32)
-    c, s = sincos_turns(shift * lane * F32(-4.0 / N))
-    hc, hs = sincos_turns(shift * F32(0.5))
-    phases[at, 0, :, 0:A] = c
-    phases[at, 1, :, 0:A] = s
-    phases[at, 0, :, A:] = c * hc - s * hs
-    phases[at, 1, :, A:] = c * hs + s * hc
+    lane = lax.broadcasted_iota(jnp.int32, (A, A), 1)
+    lane = jnp.where(lane < A // 2, lane, lane - A).astype(F32)
+    c, s = sincos_turns(shift * lane * F32(-8.0 / N))
+    phases[at, 0] = c
+    phases[at, 1] = s
     c1, s1 = sincos_turns(shift * F32(-1.0 / N))
     steps[at, 0] = c1
     steps[at, 1] = s1
 
 
-def put_split(ref, m1, signals, n, which, re, im):
-    rh, rl = split(re)
-    ih, il = split(im)
-    for part, value in enumerate((rh, ih, rl, il)):
-        base = (part // 2) * 2 * n * A + (part % 2) * n * A + which * A
-        ref[m1, base : base + A, :] = value
-
-
 def product(lhs, hi, lo, rows):
     both = dot(lhs, hi)
     return both[:rows] + both[rows:] + dot(lhs[:rows], lo)
@@ -106,62 +112,51 @@
 
 def stage(inputs, plan, zz, uu, hi_ref, lo_ref, mats, phases, steps):
     n_in, n_out = len(inputs), len(plan)
+    rows_in, rows_out = n_in * A, n_out * A
     for which, (re, im) in enumerate(inputs):
-        zr, zi = quarter_turns(re, im, -1)
-        for m1 in range(4):
-            put_split(zz, m1, None, n_in, which, zr[m1], zi[m1])
-
-    def body(m1, carry):
-        rows = 2 * n_in * A
-        p = product(zz[m1, : 2 * rows, :], hi_ref[0, m1], lo_ref[0, m1], rows)
-        half = n_in * A
-        xr = p[:half, :H] + p[half:, H:]
-        xi = p[half:, :H] - p[:half, H:]
-        stacked = []
-        for which in range(n_in):
-            x = jnp.concatenate([xr[which * A : which * A + A], xi[which * A : which * A + A]], axis=1)
-            h, l = split(x)
-            stacked.append(jnp.concatenate([h, l], axis=0))
-        parts = [[], [], [], []]
+        zr, zi = eighth_turns(re, im, -1)
+        for m1 in range(8):
+            h, l = split(jnp.concatenate([zr[m1], zi[m1]], axis=1))
+            zz[m1, which * A : which * A + A] = h
+            zz[m1, rows_in + which * A : rows_in + which * A + A] = l
+    turns = {at: (phases[at, 0], phases[at, 1]) for terms in plan for _, at in terms}
+    for m1 in range(8):
+        x = product(zz[m1, : 2 * rows_in], hi_ref[0, m1], lo_ref[0, m1], rows_in)
+        h, l = split(x)
+        stacked = [
+            jnp.concatenate([h[which * A : which * A + A], l[which * A : which * A + A]], axis=0)
+            for which in range(n_in)
+        ]
+        highs, lows = [], []
         for terms in plan:
             mr = mi = None
             for which, at in terms:
                 y = dot(mats[at], stacked[which])
                 y = y[:A] + y[A:]
-                yr, yi = y[:, :H], y[:, H:]
-                c, s = phases[at, 0], phases[at, 1]
+                yr, yi = y[:, :A], y[:, A:]
+                c, s = turns[at]
                 tr, ti = c * yr - s * yi, c * yi + s * yr
                 mr, mi = (tr, ti) if mr is None else (mr + tr, mi + ti)
-                c1, s1 = steps[at, 0], steps[at, 1]
-                c1 = jnp.concatenate([c1, c1], axis=1)
-                s1 = jnp.concatenate([s1, s1], axis=1)
-                phases[at, 0] = c * c1 - s * s1
-                phases[at, 1] = c * s1 + s * c1
-            rh, rl = split(mr)
-            ih, il = split(mi)
-            for k, v in enumerate((rh, ih, rl, il)):
-                parts[k].append(v)
-        lhs = jnp.concatenate([v for part in parts for v in part], axis=0)
-        rows = 2 * n_out * A
-        p = product(lhs, hi_ref[1, m1], lo_ref[1, m1], rows)
-        half = n_out * A
-        uu[m1, :half, :H] = p[:half, :H] - p[half:, H:]
-        uu[m1, :half, H:] = p[:half, H:] + p[half:, :H]
-        return carry
-
-    lax.fori_loop(0, 4, body, 0)
+                if m1 < 7:
+                    c1, s1 = steps[at, 0], steps[at, 1]
+                    turns[at] = (c * c1 - s * s1, c * s1 + s * c1)
+            h, l = split(jnp.concatenate([mr, mi], axis=1))
+            highs.append(h)
+            lows.append(l)
+        lhs = jnp.concatenate(highs + lows, axis=0)
+        uu[m1, :rows_out] = product(lhs, hi_ref[1, m1], lo_ref[1, m1], rows_out)
     out = []
     for which in range(n_out):
         base = which * A
-        re = [uu[m1, base : base + A, :H] for m1 in range(4)]
-        im = [uu[m1, base : base + A, H:] for m1 in range(4)]
-        out.append(quarter_turns(re, im, 1))
+        re = [uu[m1, base : base + A, :A] for m1 in range(8)]
+        im = [uu[m1, base : base + A, A:] for m1 in range(8)]
+        out.append(eighth_turns(re, im, 1))
     return out
 
 
 def gained(blocks, gain, section):
     re, im = blocks
-    rows = [gain[section : section + 1, H * k : H * k + H] * F32(1.0 / N) for k in range(4)]
+    rows = [gain[section : section + 1, A * k : A * k + A] * F32(1.0 / N) for k in range(8)]
     return [v * g for v, g in zip(re, rows)], [v * g for v, g in zip(im, rows)]
 
 
@@ -176,7 +171,7 @@
     run = functools.partial(stage, zz=zz, uu=uu, hi_ref=hi, lo_ref=lo, mats=mats, phases=phases, steps=steps)
 
     def blocks(ref):
-        return [[ref[p, :, H * k : H * k + H] for k in range(4)] for p in range(2)]
+        return [[ref[p, :, A * k : A * k + A] for k in range(8)] for p in range(2)]
 
     first = run([blocks(own), blocks(other)], [[(0, 0), (1, 1)]])
     y = gained(first[0], gain, 0)
@@ -185,14 +180,10 @@
     third = run(z, [[(0, 4)], [(1, 5)], [(0, 6)], [(1, 7)]])
     for j, v in enumerate(third):
         re, im = gained(v, gain, 2)
-        for k in range(4):
-            for part in range(2):
-                both = jnp.concatenate(
-                    [re[k][:, A * part : A * part + A], im[k][:, A * part : A * part + A]], axis=1
-                )
-                h, l = split(both)
-                out[j, 2 * k + part, 0:A] = h
-                out[j, 2 * k + part, A:] = l
+        for q in range(8):
+            h, l = split(jnp.concatenate([re[q], im[q]], axis=1))
+            out[j, q, 0:A] = h
+            out[j, q, A:] = l
 
 
 ROWS = A + 8
@@ -206,27 +197,18 @@
         return (owner % 2) * 8 + owner // 2
 
     for j, w in enumerate((w0, w1, w2, w3)):
-
-        def body(q, carry):
+        for q in range(8):
             h, l = split(w[q])
             x = cur[j, q]
-            c = dot(h, x[:A]) + dot(l, x[:A]) + dot(h, x[A:])
+            c = dot(jnp.concatenate([h, h], axis=1), x) + dot(l, x[:A])
             owner = owners[j * 8 + q]
             acc[place(owner), 0:A] += c
             top = pltpu.roll(c[A - 8 :], 4, 0)
             bottom = pltpu.roll(c[:8], 4, 0)
-
-            @pl.when(owner < 15)
-            def _():
-                acc[place(owner + 1), A:] += jnp.where(row < 4, top, 0.0)
-
-            @pl.when(owner > 0)
-            def _():
-                acc[place(owner - 1), A:] += jnp.where(row >= 4, bottom, 0.0)
-
-            return carry
-
-        lax.fori_loop(0, 8, body, 0)
+            above = jnp.maximum(owner - 1, 0)
+            below = jnp.minimum(owner + 1, 15)
+            acc[place(below), A:] += jnp.where((row < 4) & (owner < 15), top, 0.0)
+            acc[place(above), A:] += jnp.where((row >= 4) & (owner > 0), bottom, 0.0)
     mine = pl.multiple_of(bits[0] * 8, 8)
     theirs = pl.multiple_of(8 - bits[0] * 8, 8)
     keep[...] = acc[pl.ds(mine, 8)]
@@ -242,20 +224,33 @@
     for k in range(1, 8):
         total = total + parts[k]
     tile[...] = total
-    first[...] = jnp.concatenate([total[:, 0:A], total[:, A:]], axis=0)
-    last[...] = jnp.concatenate([total[:, 0:A], total[:, A:]], axis=0)
+    re, im = total[:, :A], total[:, A:]
+    lane = lax.broadcasted_iota(jnp.int32, (ROWS, A), 1)
+    for ref, edge in (
+        (first, jnp.where(lane < 4, re, pltpu.roll(im, 4, 1))),
+        (last, jnp.where(lane < 4, pltpu.roll(re, 4, 1), pltpu.roll(im, 8, 1))),
+    ):
+        ref[:, :A] = edge[:A].T[:8]
+        ends = jnp.concatenate([edge[A:], jnp.zeros((A - 8, A), F32)], axis=0)
+        ref[:, A:] = ends.T[:8]
 
 
 def filter_kernel(index, bank, tile, before, after, out, pad, moved):
     number = index[0, 0]
+    sides = []
+    for ref in (before, after):
+        blank = jnp.zeros((A - 8, A), F32)
+        main = jnp.concatenate([ref[:, :A], blank], axis=0).T
+        ends = jnp.concatenate([ref[:, A:], blank], axis=0).T
+        sides.append(jnp.concatenate([main, ends[:8]], axis=0))
+    lane = lax.broadcasted_iota(jnp.int32, (ROWS, A), 1)
     for p in range(2):
         body = tile[:, A * p : A * p + A]
-        lead = before[ROWS * p : ROWS * p + ROWS, :]
-        tail = after[ROWS * p : ROWS * p + ROWS, :]
-        lane = lax.broadcasted_iota(jnp.int32, (ROWS, A), 1)
         turned = pltpu.roll(body, 4, 1)
-        left = jnp.where(lane < 4, pltpu.roll(lead, 4, 1), turned)
-        right = jnp.where(lane < 4, turned, pltpu.roll(tail, 4, 1))
+        lead = sides[0] if p == 0 else pltpu.roll(sides[0], A - 4, 1)
+        tail = pltpu.roll(sides[1], 4, 1) if p == 0 else sides[1]
+        left = jnp.where(lane < 4, lead, turned)
+        right = jnp.where(lane < 4, turned, tail)
         for half, value in enumerate((left, right)):
             pad[4 : 4 + A, A * half : A * half + A] = value[0:A]
             pad[0:4, A * half : A * half + A] = value[A : A + 4]
@@ -314,10 +309,10 @@
         struct((4, 8, 2 * A, H), BF16),
         [SMEM] + [VMEM] * 9,
         [
-            pltpu.VMEM((4, 8 * A, H), BF16),
-            pltpu.VMEM((4, 4 * A, 2 * H), F32),
+            pltpu.VMEM((8, 4 * A, H), BF16),
+            pltpu.VMEM((8, 4 * A, H), F32),
             pltpu.VMEM((8, 2 * A, 2 * A), BF16),
-            pltpu.VMEM((8, 2, A, H), F32),
+            pltpu.VMEM((8, 2, A, A), F32),
             pltpu.VMEM((8, 2, A, A), F32),
         ],
         flops=12 * 10**9,
@@ -335,7 +330,7 @@
     groups = [[c + 2 * k for k in range(8)] for c in range(2)]
     parts = lax.all_to_all(half, "aper", split_axis=0, concat_axis=0, axis_index_groups=groups, tiled=True)
     tile, first, last = call(
-        tile_kernel, (struct((ROWS, H)), struct((2 * ROWS, A)), struct((2 * ROWS, A))), [VMEM]
+        tile_kernel, (struct((ROWS, H)), struct((8, H)), struct((8, H))), [VMEM]
     )(parts)
     before = lax.ppermute(last, "swath", [(i, i + 1) for i in range(7)])
     after = lax.ppermute(first, "swath", [(i + 1, i) for i in range(7)])

time: 107 us -> 85.6 us (0.80)
  Pallas kernels: 45 us -> 25 us
  waiting for transfers between devices: 11.8 us -> 10.4 us
    pallas_call x1, Pallas kernels: 32.8 us -> 18.3 us  [shards(): call(merge_kernel, struct((4, 8, 2 * A, H), BF16), [SMEM] + [VMEM] * 9, [...]
    pallas_call x1, Pallas kernels: 9.52 us -> 3.86 us  [shards(): call(contrib_kernel, (struct((8, ROWS, H)), struct((8, ROWS, H))), [SMEM,...]
    ppermute x1, waiting for transfers between devices: 1.3 us -> 0.01 us  [shards(): before = lax.ppermute(last, 'swath', [(i, i + 1) for i in range(7)])]
  transfers between devices with their start and end apart: 10 -> 10, of which waited for: 4 -> 3; matrix products, arithmetic and copies ran while one was open for 4% -> 5% of each run, Pallas kernels for 31% -> 22%
where the time goes in v2:
time: 85.6 us; the launch traced here: 85.1 us
  Pallas kernels  25 us (29%)
  blocking collectives  24.3 us (28%)
  starting transfers between devices  16.6 us (19%)
  waiting for transfers between devices  10.4 us (12%)
  local copies, waits for them, and re-layouts  4.31 us (5%)
  other arithmetic  3.74 us (4%)
    all_to_all x1, blocking collectives, shards(): lax.all_to_all(half, 'aper', split_axis=0, concat_axis=0, axis_index_grou...  24.3 us
    pallas_call x1, Pallas kernels, shards(): call(merge_kernel, struct((4, 8, 2 * A, H), BF16), [SMEM] + [VMEM] * 9, [...  18.3 us
    ppermute x8, starting transfers between devices, swap(): return lax.ppermute(value, 'aper', [(i, i ^ mask) for i in range(16)])  9.67 us
    ppermute x8, waiting for transfers between devices, swap(): return lax.ppermute(value, 'aper', [(i, i ^ mask) for i in range(16)])  6.5 us
    ppermute x1, starting transfers between devices, shards(): before = lax.ppermute(last, 'swath', [(i, i + 1) for i in range(7)])  4.99 us
    pallas_call x1, Pallas kernels, shards(): call(contrib_kernel, (struct((8, ROWS, H)), struct((8, ROWS, H))), [SMEM,...  3.86 us
    ppermute x1, waiting for transfers between devices, shards(): after = lax.ppermute(first, 'swath', [(i + 1, i) for i in range(7)])  3.86 us
    unnamed x10, local copies, waits for them, and re-layouts  3.6 us
  transfers between devices with their start and end apart: 10, of which 3 were waited for; matrix products, arithmetic and copies ran while one was open for 5% of the time, Pallas kernels for 22%

profile of v2, /device:TPU:34, one launch (start us, length us, event | category | flops | bytes accessed | tf_op | source)
XLA Modules:
  0.0 85.1 jit_solution(4551325062974555430)
XLA Ops:
  0.0 0.6 compare_reduce_fusion
  0.6 1.3 %fusion = f32[8]{0:T(128)S(1)} fusion(pred[]{:T(512)} %compare_reduce_fusion, s32[1,1,8,1]{2,3,1,0:T(1,128)} %param.18), kind=kLoop, calls=%fused_computation.3 | loop fusion | flops 16 | bytes 65 | tf_op jit(solution)/shard_map/squeeze | solution.py:320
  1.9 0.7 convert_element_type.19
  2.7 0.7 broadcast_in_dim.6
  3.4 0.8 pad_maximum_fusion.tab
  4.2 2.2 %collective-permute-start = (f32[6,24,128]{2,1,0:T(8,128)S(1)}, f32[6,24,128]{2,1,0:T(8,128)S(1)}, u32[]{:S(2)}, u32[]{:S(2)}) collective-permute-start(f32[6,24,128]{2,1,0:T(8,128)S(1)} %pad_maximum_fusion.tab), channel_id=1, source_target_pairs={{0,16},{8,24},{16,0},{24,8},{32,48},{40,56},{48,32},{56,40},{64,80... | collective-permute-start | bytes 221192 | tf_op jit(solution)/shard_map/ppermute | solution.py:286
  6.4 1.6 %collective-permute-start.1 = (f32[6,24,128]{2,1,0:T(8,128)S(1)}, f32[6,24,128]{2,1,0:T(8,128)S(1)}, u32[]{:S(2)}, u32[]{:S(2)}) collective-permute-start(f32[6,24,128]{2,1,0:T(8,128)S(1)} %pad_maximum_fusion.tab), channel_id=1, source_target_pairs={{0,32},{8,40},{16,48},{24,56},{32,0},{40,8},{48,16},{56,24},{64,96... | collective-permute-start | bytes 221192 | tf_op jit(solution)/shard_map/ppermute | solution.py:286
  7.9 1.3 %collective-permute-start.2 = (f32[6,24,128]{2,1,0:T(8,128)S(1)}, f32[6,24,128]{2,1,0:T(8,128)S(1)}, u32[]{:S(2)}, u32[]{:S(2)}) collective-permute-start(f32[6,24,128]{2,1,0:T(8,128)S(1)} %pad_maximum_fusion.tab), channel_id=1, source_target_pairs={{0,48},{8,56},{16,32},{24,40},{32,16},{40,24},{48,0},{56,8},{64,11... | collective-permute-start | bytes 221192 | tf_op jit(solution)/shard_map/ppermute | solution.py:286
  9.2 2.1 %collective-permute-start.4 = (f32[8,128,128]{2,1,0:T(8,128)}, f32[8,128,128]{2,1,0:T(8,128)S(1)}, u32[]{:S(2)}, u32[]{:S(2)}) collective-permute-start(f32[8,128,128]{2,1,0:T(8,128)} %bitcast.14), channel_id=1, source_target_pairs={{0,16},{8,24},{16,0},{24,8},{32,48},{40,56},{48,32},{56,40},{64,80... | collective-permute-start | bytes 1572872 | tf_op jit(solution)/shard_map/ppermute | solution.py:286
  11.4 3.7 %collective-permute-done.2.tabd = f32[6,24,128]{2,1,0:T(8,128)S(1)} collective-permute-done((f32[6,24,128]{2,1,0:T(8,128)S(1)}, f32[6,24,128]{2,1,0:T(8,128)S(1)}, u32[]{:S(2)}, u32[]{:S(2)}) %collective-permute-start.2) | collective-permute-done | bytes 73760 | tf_op jit(solution)/shard_map/ppermute | solution.py:286
  15.2 0.4 collective-permute-start.5
  15.6 1.9 %collective-permute-start.6 = (f32[8,128,128]{2,1,0:T(8,128)}, f32[8,128,128]{2,1,0:T(8,128)S(1)}, u32[]{:S(2)}, u32[]{:S(2)}) collective-permute-start(f32[8,128,128]{2,1,0:T(8,128)} %bitcast.16), channel_id=1, source_target_pairs={{0,48},{8,56},{16,32},{24,40},{32,16},{40,24},{48,0},{56,8},{64,11... | collective-permute-start | bytes 1572872 | tf_op jit(solution)/shard_map/ppermute | solution.py:286
  17.7 1.3 %copy-done.2 = f32[2,128,1024]{2,1,0:T(8,128)S(1)} copy-done((f32[2,128,1024]{2,1,0:T(8,128)S(1)}, f32[2,128,1024]{2,1,0:T(8,128)}, u32[]{:S(2)}) %copy-start.2) | copy-done | bytes 1048600
  19.0 0.7 copy-done.3
  19.7 1.6 %copy-done.4 = bf16[2,8,256,256]{3,2,1,0:T(8,128)(2,1)S(1)} copy-done((bf16[2,8,256,256]{3,2,1,0:T(8,128)(2,1)S(1)}, bf16[2,8,256,256]{3,2,1,0:T(8,128)(2,1)}, u32[]{:S(2)}) %copy-start.4) | copy-done | bytes 2097176
  21.3 18.3 %shard_map.109.cur = bf16[4,8,256,256]{3,2,1,0:T(8,128)(2,1)} custom-call(s32[3]{0:T(128)S(1)} %pad_add_fusion.bits, f32[2,128,1024]{2,1,0:T(8,128)S(1)} %copy-done.2, f32[2,128,1024]{2,1,0:T(8,128)S(1)} %collective-permute-done.3.other, f32[6,24,128]{2,1,0:T(8,128)S(1)} %pad_maximum_fusion.tab, f32[6,24,128]{2,1,0:T(8,128)S(1)} %collective-permute-done.tabx, ...), custom_call_target="tpu_custom_call" | custom-call | flops 12000000000 | bytes 1048576 | tf_op jit(solution)/shard_map/pallas_call | solution.py:307
  39.6 3.9 %shard_map.110 = (f32[8,136,256]{2,1,0:T(8,128)S(1)}, f32[8,136,256]{2,1,0:T(8,128)S(1)}) custom-call(s32[32]{0:T(128)S(1)} %maximum_convert_fusion.owners, s32[3]{0:T(128)S(1)} %pad_add_fusion.bits, bf16[4,8,256,256]{3,2,1,0:T(8,128)(2,1)} %shard_map.109.cur, f32[8,128,128]{2,1,0:T(8,128)S(1)} %bitcast.17, f32[8,128,128]{2,1,0:T(8,128)S(1)} %collective-permute-done.4.w1, ...), custom_call_target="tpu_custom_call" | custom-call | flops 1000000000 | bytes 1048576 | tf_op jit(solution)/shard_map/pallas_call | solution.py:321
  43.5 2.7 %collective-permute-done.7 = f32[8,136,256]{2,1,0:T(8,128)S(1)} collective-permute-done((f32[8,136,256]{2,1,0:T(8,128)S(1)}, f32[8,136,256]{2,1,0:T(8,128)S(1)}, u32[]{:S(2)}, u32[]{:S(2)}) %collective-permute-start.7) | collective-permute-done | bytes 1114144 | tf_op jit(solution)/shard_map/ppermute | solution.py:286
  46.4 24.3 %all_to_all.5.parts = f32[8,136,256]{2,1,0:T(8,128)S(1)} all-to-all(f32[8,136,256]{2,1,0:T(8,128)S(1)} %add.22), channel_id=1, replica_groups={{0,16,32,48,64,80,96,112},{8,24,40,56,72,88,104,120},{1,17,33,49,65,81,..., dimensions={0} | all-to-all | bytes 2228224 | tf_op jit(solution)/shard_map/all_to_all | solution.py:331
  70.8 0.2 shard_map.111
  71.0 5.0 %collective-permute-start.8 = (f32[8,256]{1,0:T(8,128)S(1)}, f32[8,256]{1,0:T(8,128)S(1)}, u32[]{:S(2)}, u32[]{:S(2)}) collective-permute-start(f32[8,256]{1,0:T(8,128)S(1)} %get-tuple-element.25), channel_id=1, source_target_pairs={{0,1},{1,2},{2,3},{3,4},{4,5},{5,6},{6,7},{8,9},{9,10},{10,11},{11... | collective-permute-start | bytes 24584 | tf_op jit(solution)/shard_map/ppermute | solution.py:335
  76.0 1.9 %collective-permute-start.9 = (f32[8,256]{1,0:T(8,128)S(1)}, f32[8,256]{1,0:T(8,128)S(1)}, u32[]{:S(2)}, u32[]{:S(2)}) collective-permute-start(f32[8,256]{1,0:T(8,128)S(1)} %get-tuple-element.26), channel_id=1, source_target_pairs={{1,0},{2,1},{3,2},{4,3},{5,4},{6,5},{7,6},{9,8},{10,9},{11,10},{12... | collective-permute-start | bytes 24584 | tf_op jit(solution)/shard_map/ppermute | solution.py:336
  78.6 3.9 %collective-permute-done.9.after = f32[8,256]{1,0:T(8,128)S(1)} collective-permute-done((f32[8,256]{1,0:T(8,128)S(1)}, f32[8,256]{1,0:T(8,128)S(1)}, u32[]{:S(2)}, u32[]{:S(2)}) %collective-permute-start.9) | collective-permute-done | bytes 8224 | tf_op jit(solution)/shard_map/ppermute | solution.py:336
  82.4 2.6 %shard_map.112 = f32[2,128,128]{2,1,0:T(8,128)} custom-call(s32[1,1]{1,0:T(1,128)S(6)} %copy.12.index, f32[16,81]{1,0:T(8,128)S(1)} %copy-done.1, f32[136,256]{1,0:T(8,128)S(1)} %get-tuple-element.24.tile, f32[8,256]{1,0:T(8,128)S(1)} %collective-permute-done.8.before, f32[8,256]{1,0:T(8,128)S(1)} %collective-permute-done.9.after), custom_call_target="tpu_custom_call" | custom-call | flops 1000000 | bytes 1048576 | tf_op jit(solution)/shard_map/pallas_call | solution.py:337
  (25 shorter events, 0.4 us)
Async XLA Ops:
  0.0 17.7 %collective-permute-start.3 = (f32[2,128,1024]{2,1,0:T(8,128)}, f32[2,128,1024]{2,1,0:T(8,128)S(1)}, u32[]{:S(2)}, u32[]{:S(2)}) collective-permute-start(f32[2,128,1024]{2,1,0:T(8,128)} %own.1), channel_id=1, source_target_pairs={{0,8},{8,0},{16,24},{24,16},{32,40},{40,32},{48,56},{56,48},{64,72... | collective-permute-start | bytes 3145736 | tf_op jit(solution)/shard_map/ppermute | solution.py:286
  4.2 13.4 %collective-permute-start = (f32[6,24,128]{2,1,0:T(8,128)S(1)}, f32[6,24,128]{2,1,0:T(8,128)S(1)}, u32[]{:S(2)}, u32[]{:S(2)}) collective-permute-start(f32[6,24,128]{2,1,0:T(8,128)S(1)} %pad_maximum_fusion.tab), channel_id=1, source_target_pairs={{0,16},{8,24},{16,0},{24,8},{32,48},{40,56},{48,32},{56,40},{64,80... | collective-permute-start | bytes 221192 | tf_op jit(solution)/shard_map/ppermute | solution.py:286
  6.4 9.3 %collective-permute-start.1 = (f32[6,24,128]{2,1,0:T(8,128)S(1)}, f32[6,24,128]{2,1,0:T(8,128)S(1)}, u32[]{:S(2)}, u32[]{:S(2)}) collective-permute-start(f32[6,24,128]{2,1,0:T(8,128)S(1)} %pad_maximum_fusion.tab), channel_id=1, source_target_pairs={{0,32},{8,40},{16,48},{24,56},{32,0},{40,8},{48,16},{56,24},{64,96... | collective-permute-start | bytes 221192 | tf_op jit(solution)/shard_map/ppermute | solution.py:286
  7.9 7.2 %collective-permute-start.2 = (f32[6,24,128]{2,1,0:T(8,128)S(1)}, f32[6,24,128]{2,1,0:T(8,128)S(1)}, u32[]{:S(2)}, u32[]{:S(2)}) collective-permute-start(f32[6,24,128]{2,1,0:T(8,128)S(1)} %pad_maximum_fusion.tab), channel_id=1, source_target_pairs={{0,48},{8,56},{16,32},{24,40},{32,16},{40,24},{48,0},{56,8},{64,11... | collective-permute-start | bytes 221192 | tf_op jit(solution)/shard_map/ppermute | solution.py:286
  9.2 30.3 %collective-permute-start.4 = (f32[8,128,128]{2,1,0:T(8,128)}, f32[8,128,128]{2,1,0:T(8,128)S(1)}, u32[]{:S(2)}, u32[]{:S(2)}) collective-permute-start(f32[8,128,128]{2,1,0:T(8,128)} %bitcast.14), channel_id=1, source_target_pairs={{0,16},{8,24},{16,0},{24,8},{32,48},{40,56},{48,32},{56,40},{64,80... | collective-permute-start | bytes 1572872 | tf_op jit(solution)/shard_map/ppermute | solution.py:286
  15.2 24.4 %collective-permute-start.5 = (f32[8,128,128]{2,1,0:T(8,128)}, f32[8,128,128]{2,1,0:T(8,128)S(1)}, u32[]{:S(2)}, u32[]{:S(2)}) collective-permute-start(f32[8,128,128]{2,1,0:T(8,128)} %bitcast.15), channel_id=1, source_target_pairs={{0,32},{8,40},{16,48},{24,56},{32,0},{40,8},{48,16},{56,24},{64,96... | collective-permute-start | bytes 1572872 | tf_op jit(solution)/shard_map/ppermute | solution.py:286
  15.6 24.0 %collective-permute-start.6 = (f32[8,128,128]{2,1,0:T(8,128)}, f32[8,128,128]{2,1,0:T(8,128)S(1)}, u32[]{:S(2)}, u32[]{:S(2)}) collective-permute-start(f32[8,128,128]{2,1,0:T(8,128)} %bitcast.16), channel_id=1, source_target_pairs={{0,48},{8,56},{16,32},{24,40},{32,16},{40,24},{48,0},{56,8},{64,11... | collective-permute-start | bytes 1572872 | tf_op jit(solution)/shard_map/ppermute | solution.py:286
  17.7 21.9 %copy-start = (f32[1,1,8,128,128]{4,3,2,1,0:T(8,128)S(1)}, f32[1,1,8,128,128]{4,3,2,1,0:T(8,128)}, u32[]{:S(2)}) copy-start(f32[1,1,8,128,128]{4,3,2,1,0:T(8,128)} %param.19) | copy-start | bytes 1572868
  17.7 1.3 %copy-start.2 = (f32[2,128,1024]{2,1,0:T(8,128)S(1)}, f32[2,128,1024]{2,1,0:T(8,128)}, u32[]{:S(2)}) copy-start(f32[2,128,1024]{2,1,0:T(8,128)} %own.1) | copy-start | bytes 3145732
  19.0 0.7 copy-start.3
  19.7 1.6 %copy-start.4 = (bf16[2,8,256,256]{3,2,1,0:T(8,128)(2,1)S(1)}, bf16[2,8,256,256]{3,2,1,0:T(8,128)(2,1)}, u32[]{:S(2)}) copy-start(bf16[2,8,256,256]{3,2,1,0:T(8,128)(2,1)} %constant.82.clone.hi) | copy-start | bytes 6291460
  43.5 2.8 %collective-permute-start.7 = (f32[8,136,256]{2,1,0:T(8,128)S(1)}, f32[8,136,256]{2,1,0:T(8,128)S(1)}, u32[]{:S(2)}, u32[]{:S(2)}) collective-permute-start(f32[8,136,256]{2,1,0:T(8,128)S(1)} %get-tuple-element.23), channel_id=1, source_target_pairs={{0,8},{8,0},{16,24},{24,16},{32,40},{40,32},{48,56},{56,48},{64,72... | collective-permute-start | bytes 3342344 | tf_op jit(solution)/shard_map/ppermute | solution.py:286
  70.8 11.7 %copy-start.1 = (f32[16,81]{1,0:T(8,128)S(1)}, f32[16,81]{1,0:T(8,128)}, u32[]{:S(2)}) copy-start(f32[16,81]{1,0:T(8,128)} %bank.1) | copy-start | bytes 15556
  71.0 7.6 %collective-permute-start.8 = (f32[8,256]{1,0:T(8,128)S(1)}, f32[8,256]{1,0:T(8,128)S(1)}, u32[]{:S(2)}, u32[]{:S(2)}) collective-permute-start(f32[8,256]{1,0:T(8,128)S(1)} %get-tuple-element.25), channel_id=1, source_target_pairs={{0,1},{1,2},{2,3},{3,4},{4,5},{5,6},{6,7},{8,9},{9,10},{10,11},{11... | collective-permute-start | bytes 24584 | tf_op jit(solution)/shard_map/ppermute | solution.py:335
  76.0 6.4 %collective-permute-start.9 = (f32[8,256]{1,0:T(8,128)S(1)}, f32[8,256]{1,0:T(8,128)S(1)}, u32[]{:S(2)}, u32[]{:S(2)}) collective-permute-start(f32[8,256]{1,0:T(8,128)S(1)} %get-tuple-element.26), channel_id=1, source_target_pairs={{1,0},{2,1},{3,2},{4,3},{5,4},{6,5},{7,6},{9,8},{10,9},{11,10},{12... | collective-permute-start | bytes 24584 | tf_op jit(solution)/shard_map/ppermute | solution.py:336

commit v3 on v2

--- a/solution.py
+++ b/solution.py
@@ -15,6 +15,7 @@
 F32 = jnp.float32
 BF16 = jnp.bfloat16
 VMEM = pl.BlockSpec(memory_space=pltpu.VMEM)
+HBM = pl.BlockSpec(memory_space=pltpu.HBM)
 SMEM = pl.BlockSpec(memory_space=pltpu.SMEM)
 
 
@@ -26,11 +27,11 @@
         angle = 2.0 * np.pi * ((r * m) % N) / N
         c, s = np.cos(angle), np.sin(angle)
         forward = np.block([[c, -s], [s, c]])
-        out.append(np.stack([forward, forward.T]))
-    full = np.stack(out, 1).astype(np.float32)
+        out.append(forward)
+    full = np.stack(out).astype(np.float32)
     hi = full.astype(jnp.bfloat16)
     lo = (full - hi.astype(np.float32)).astype(jnp.bfloat16)
-    return hi, lo
+    return np.stack([hi, lo])
 
 
 def split(x):
@@ -105,12 +106,15 @@
     steps[at, 1] = s1
 
 
-def product(lhs, hi, lo, rows):
-    both = dot(lhs, hi)
-    return both[:rows] + both[rows:] + dot(lhs[:rows], lo)
-
-
-def stage(inputs, plan, zz, uu, hi_ref, lo_ref, mats, phases, steps):
+def product(lhs, table, m1, rows, dims):
+    def by(a, b):
+        return lax.dot_general(a, b, (dims, ((), ())), preferred_element_type=F32)
+
+    both = by(lhs, table[0, m1])
+    return both[:rows] + both[rows:] + by(lhs[:rows], table[1, m1])
+
+
+def stage(inputs, plan, zz, uu, table, mats, phases, steps):
     n_in, n_out = len(inputs), len(plan)
     rows_in, rows_out = n_in * A, n_out * A
     for which, (re, im) in enumerate(inputs):
@@ -121,7 +125,7 @@
             zz[m1, rows_in + which * A : rows_in + which * A + A] = l
     turns = {at: (phases[at, 0], phases[at, 1]) for terms in plan for _, at in terms}
     for m1 in range(8):
-        x = product(zz[m1, : 2 * rows_in], hi_ref[0, m1], lo_ref[0, m1], rows_in)
+        x = product(zz[m1, : 2 * rows_in], table, m1, rows_in, ((1,), (0,)))
         h, l = split(x)
         stacked = [
             jnp.concatenate([h[which * A : which * A + A], l[which * A : which * A + A]], axis=0)
@@ -144,7 +148,7 @@
             highs.append(h)
             lows.append(l)
         lhs = jnp.concatenate(highs + lows, axis=0)
-        uu[m1, :rows_out] = product(lhs, hi_ref[1, m1], lo_ref[1, m1], rows_out)
+        uu[m1, :rows_out] = product(lhs, table, m1, rows_out, ((1,), (1,)))
     out = []
     for which in range(n_out):
         base = which * A
@@ -160,7 +164,15 @@
     return [v * g for v, g in zip(re, rows)], [v * g for v, g in zip(im, rows)]
 
 
-def merge_kernel(bits, own, other, tab, tabx, taby, tabd, gain, hi, lo, out, zz, uu, mats, phases, steps):
+def merge_kernel(
+    bits, other, tab, tabx, taby, tabd, own_in, gain_in, table_in, out, zz, uu, mats, phases, steps, own, gain, table, sems
+):
+    copies = [
+        pltpu.make_async_copy(source, target, sems.at[k])
+        for k, (source, target) in enumerate(((own_in, own), (table_in, table), (gain_in, gain)))
+    ]
+    for copy in copies:
+        copy.start()
     b0, b1, b2 = bits[0], bits[1], bits[2]
     prepare(tab[b0], 0, mats, phases, steps)
     prepare(tab[1 - b0], 1, mats, phases, steps)
@@ -168,11 +180,13 @@
     prepare(tabx[2 + b1], 3, mats, phases, steps)
     for at, ref in ((4, tab), (5, tabx), (6, taby), (7, tabd)):
         prepare(ref[4 + b2], at, mats, phases, steps)
-    run = functools.partial(stage, zz=zz, uu=uu, hi_ref=hi, lo_ref=lo, mats=mats, phases=phases, steps=steps)
+    run = functools.partial(stage, zz=zz, uu=uu, table=table, mats=mats, phases=phases, steps=steps)
 
     def blocks(ref):
         return [[ref[p, :, A * k : A * k + A] for k in range(8)] for p in range(2)]
 
+    for copy in copies:
+        copy.wait()
     first = run([blocks(own), blocks(other)], [[(0, 0), (1, 1)]])
     y = gained(first[0], gain, 0)
     second = run([y], [[(0, 2)], [(0, 3)]])
@@ -194,7 +208,8 @@
     row = lax.broadcasted_iota(jnp.int32, (8, H), 0)
 
     def place(owner):
-        return (owner % 2) * 8 + owner // 2
+        apart = owner ^ bits[3]
+        return (apart & 1) * 8 + (apart >> 1)
 
     for j, w in enumerate((w0, w1, w2, w3)):
         for q in range(8):
@@ -209,20 +224,35 @@
             below = jnp.minimum(owner + 1, 15)
             acc[place(below), A:] += jnp.where((row < 4) & (owner < 15), top, 0.0)
             acc[place(above), A:] += jnp.where((row >= 4) & (owner > 0), bottom, 0.0)
-    mine = pl.multiple_of(bits[0] * 8, 8)
-    theirs = pl.multiple_of(8 - bits[0] * 8, 8)
-    keep[...] = acc[pl.ds(mine, 8)]
-    send[...] = acc[pl.ds(theirs, 8)]
-
-
-def add_kernel(a, b, out):
-    out[...] = a[...] + b[...]
-
-
-def tile_kernel(parts, tile, first, last):
-    total = parts[0]
-    for k in range(1, 8):
-        total = total + parts[k]
+    keep[...] = acc[0:8]
+    send[...] = acc[8:]
+
+
+def halves_kernel(keep, taken, g0, g1, g2, g3):
+    for k, ref in enumerate((g0, g1, g2, g3)):
+        ref[...] = keep[2 * k : 2 * k + 2] + taken[2 * k : 2 * k + 2]
+
+
+def rows_kernel(g0, r1, r2, r3, mine, theirs):
+    for k, ref in enumerate((mine, theirs)):
+        ref[...] = (g0[k] + r1[k]) + (r2[k] + r3[k])
+
+
+def table_kernel(owners, index, weight, shift, out):
+    lane = lax.broadcasted_iota(jnp.int32, (4, A), 1)
+    row = jnp.zeros((4, A), jnp.int32)
+    for q in range(8):
+        row = jnp.where(lane == q, owners[q], row)
+    for k in range(6):
+        section, child = k // 2, k % 2
+        out[k, 0:8] = index[section, 0, child].astype(F32)
+        out[k, 8:16] = weight[section, 0, child]
+        out[k, 16:20] = jnp.broadcast_to(shift[section, 0, child : child + 1, :], (4, A))
+        out[k, 20:24] = row.astype(F32)
+
+
+def tile_kernel(mine, taken, tile, first, last):
+    total = mine[...] + taken[...]
     tile[...] = total
     re, im = total[:, :A], total[:, A:]
     lane = lax.broadcasted_iota(jnp.int32, (ROWS, A), 1)
@@ -266,14 +296,14 @@
         out[p] = total
 
 
-def call(kernel, out_shape, in_specs, scratch=(), flops=1000000):
+def call(kernel, out_shape, in_specs, scratch=(), flops=1000000, limit=16):
     return pl.pallas_call(
         kernel,
         out_shape=out_shape,
         in_specs=in_specs,
         out_specs=jax.tree.map(lambda _: VMEM, out_shape),
         scratch_shapes=list(scratch),
-        compiler_params=pltpu.CompilerParams(vmem_limit_bytes=48 << 20),
+        compiler_params=pltpu.CompilerParams(vmem_limit_bytes=limit << 20),
         cost_estimate=pl.CostEstimate(flops=flops, bytes_accessed=1 << 20, transcendentals=0),
     )
 
@@ -287,36 +317,34 @@
 
 
 def shards(polar, tap_index, tap_weight, range_shift, range_gain, tile_owner, weights, kernel_index, bank):
-    place = lax.axis_index("aper")
-    bits = jnp.stack([place % 2, place // 2 % 2, place // 4 % 2]).astype(jnp.int32)
-    owner_row = jnp.zeros((8, A), F32).at[:, 0:8].set(tile_owner[0, 0, :, 0].astype(F32)[None, :])
-    tab = jnp.concatenate(
-        [
-            tap_index[:, 0].astype(F32),
-            tap_weight[:, 0],
-            jnp.broadcast_to(range_shift[:, 0, :, None, :], (3, 2, 4, A)),
-            jnp.broadcast_to(owner_row[0:4], (3, 2, 4, A)),
-        ],
-        axis=2,
-    ).reshape(6, 24, A)
-    tabx, taby, tabd = (swap(tab, mask) for mask in (2, 4, 6))
-    other = swap(polar, 1)
+    place = lax.axis_index("aper").astype(jnp.int32)
+    bits = jnp.stack([place & 1, (place >> 1) & 1, (place >> 2) & 1, place])
     own_weights = weights[0, 0]
     wx, wy, wd = (swap(own_weights, mask) for mask in (2, 4, 6))
-    hi, lo = dft_tables()
+    tab = call(table_kernel, struct((6, 24, A)), [SMEM] + [VMEM] * 3, limit=60)(
+        tile_owner.reshape(8), tap_index, tap_weight, range_shift
+    )
+    tabx, taby, tabd = (swap(tab, mask) for mask in (2, 4, 6))
+    tabx, late = lax.optimization_barrier((tabx, polar))
+    other = swap(late, 1)
     cur = call(
         merge_kernel,
         struct((4, 8, 2 * A, H), BF16),
-        [SMEM] + [VMEM] * 9,
+        [SMEM] + [VMEM] * 5 + [HBM] * 3,
         [
             pltpu.VMEM((8, 4 * A, H), BF16),
             pltpu.VMEM((8, 4 * A, H), F32),
             pltpu.VMEM((8, 2 * A, 2 * A), BF16),
             pltpu.VMEM((8, 2, A, A), F32),
             pltpu.VMEM((8, 2, A, A), F32),
+            pltpu.VMEM((2, A, N), F32),
+            pltpu.VMEM((3, N), F32),
+            pltpu.VMEM((2, 8, H, H), BF16),
+            pltpu.SemaphoreType.DMA((3,)),
         ],
         flops=12 * 10**9,
-    )(bits, polar, other, tab, tabx, taby, tabd, range_gain, jnp.asarray(hi), jnp.asarray(lo))
+        limit=32,
+    )(bits, other, tab, tabx, taby, tabd, polar, range_gain, jnp.asarray(dft_tables()))
     owners = jnp.concatenate([t[0, 20, 0:8] for t in (tab, tabx, taby, tabd)]).astype(jnp.int32)
     keep, send = call(
         contrib_kernel,
@@ -326,12 +354,13 @@
         flops=10**9,
     )(owners, bits, cur, own_weights, wx, wy, wd)
     taken = swap(send, 1)
-    half = keep + taken
-    groups = [[c + 2 * k for k in range(8)] for c in range(2)]
-    parts = lax.all_to_all(half, "aper", split_axis=0, concat_axis=0, axis_index_groups=groups, tiled=True)
+    g0, g1, g2, g3 = call(halves_kernel, (struct((2, ROWS, H)),) * 4, [VMEM] * 2)(keep, taken)
+    r1, r2, r3 = swap(g1, 4), swap(g2, 8), swap(g3, 12)
+    mine, theirs = call(rows_kernel, (struct((ROWS, H)),) * 2, [VMEM] * 4)(g0, r1, r2, r3)
+    taken = swap(theirs, 2)
     tile, first, last = call(
-        tile_kernel, (struct((ROWS, H)), struct((8, H)), struct((8, H))), [VMEM]
-    )(parts)
+        tile_kernel, (struct((ROWS, H)), struct((8, H)), struct((8, H))), [VMEM] * 2
+    )(mine, taken)
     before = lax.ppermute(last, "swath", [(i, i + 1) for i in range(7)])
     after = lax.ppermute(first, "swath", [(i + 1, i) for i in range(7)])
     return call(

time: 85.6 us -> 77.9 us (0.910)
  blocking collectives: 24.3 us -> 0 us
  waiting for transfers between devices: 10.4 us -> 25 us
  starting transfers between devices: 16.6 us -> 22.9 us
  other arithmetic: 3.74 us -> 0.16 us
  Pallas kernels: 25 us -> 22.7 us
  local copies, waits for them, and re-layouts: 4.31 us -> 5.19 us
    all_to_all x1 -> x0, blocking collectives: 24.3 us -> none  [shards(): lax.all_to_all(half, 'aper', split_axis=0, concat_axis=0, axis_index_grou...]
    ppermute x8 -> x12, waiting for transfers between devices: 6.5 us -> 21.6 us  [swap(): return lax.ppermute(value, 'aper', [(i, i ^ mask) for i in range(16)])]
    ppermute x8 -> x12, starting transfers between devices: 9.67 us -> 17 us  [swap(): return lax.ppermute(value, 'aper', [(i, i ^ mask) for i in range(16)])]
    pallas_call x1, Pallas kernels: 3.86 us -> 2.14 us  [shards(): call(contrib_kernel, (struct((8, ROWS, H)), struct((8, ROWS, H))), [SMEM,...]
    ppermute x1, starting transfers between devices: 4.99 us -> 3.53 us  [shards(): before = lax.ppermute(last, 'swath', [(i, i + 1) for i in range(7)])]
    squeeze x1 -> x0, other arithmetic: 1.3 us -> none  [shards(): t[0, 20, 0:8]]
    unnamed x10 -> x12, local copies, waits for them, and re-layouts: 3.6 us -> 4.48 us
    pallas_call x1 -> x4, Pallas kernels: 18.3 us -> 17.7 us  [the longest x1 16.1 us: shards(): call(merge_kernel, struct((4, 8, 2 * A, H), BF16), [SMEM] + [VMEM] * 5 +...]
  transfers between devices with their start and end apart: 10 -> 14, of which waited for: 3 -> 7; matrix products, arithmetic and copies ran while one was open for 5% -> 1% of each run, Pallas kernels for 22% -> 21%
where the time goes in v3:
time: 77.9 us; the launch traced here: 76.7 us
  waiting for transfers between devices  25 us (32%)
  starting transfers between devices  22.9 us (29%)
  Pallas kernels  22.7 us (29%)
  local copies, waits for them, and re-layouts  5.19 us (7%)
    ppermute x12, waiting for transfers between devices, swap(): return lax.ppermute(value, 'aper', [(i, i ^ mask) for i in range(16)])  21.6 us
    ppermute x12, starting transfers between devices, swap(): return lax.ppermute(value, 'aper', [(i, i ^ mask) for i in range(16)])  17 us
    pallas_call x1, Pallas kernels, shards(): call(merge_kernel, struct((4, 8, 2 * A, H), BF16), [SMEM] + [VMEM] * 5 +...  16.1 us
    unnamed x12, local copies, waits for them, and re-layouts  4.48 us
    ppermute x1, starting transfers between devices, shards(): before = lax.ppermute(last, 'swath', [(i, i + 1) for i in range(7)])  3.53 us
    ppermute x1, waiting for transfers between devices, shards(): after = lax.ppermute(first, 'swath', [(i + 1, i) for i in range(7)])  3.47 us
    pallas_call x1, Pallas kernels, shards(): call(filter_kernel, struct((2, A, A)), [SMEM, SMEM] + [VMEM] * 3, [pltpu....  2.64 us
    ppermute x1, starting transfers between devices, shards(): after = lax.ppermute(first, 'swath', [(i + 1, i) for i in range(7)])  2.31 us
  transfers between devices with their start and end apart: 14, of which 7 were waited for; matrix products, arithmetic and copies ran while one was open for 1% of the time, Pallas kernels for 21%

profile of v3, /device:TPU:34, one launch (start us, length us, event | category | flops | bytes accessed | tf_op | source)
XLA Modules:
  0.0 76.7 jit_solution(3604626661355807903)
XLA Ops:
  0.0 1.4 %shard_map.100.tab = f32[6,24,128]{2,1,0:T(8,128)} custom-call(s32[8]{0:T(128)} %bitcast.18, s32[3,1,2,8,128]{4,3,2,1,0:T(8,128)} %index.2, f32[3,1,2,8,128]{4,3,2,1,0:T(8,128)} %weight.1, f32[3,1,2,128]{3,2,1,0:T(2,128)} %shift.1), custom_call_target="tpu_custom_call" | custom-call | flops 1000000 | bytes 1048576 | tf_op jit(solution)/shard_map/pallas_call | solution.py:324
  1.4 2.1 %collective-permute-start = (f32[6,24,128]{2,1,0:T(8,128)}, f32[6,24,128]{2,1,0:T(8,128)S(1)}, u32[]{:S(2)}, u32[]{:S(2)}) collective-permute-start(f32[6,24,128]{2,1,0:T(8,128)} %shard_map.100.tab), channel_id=1, source_target_pairs={{0,16},{8,24},{16,0},{24,8},{32,48},{40,56},{48,32},{56,40},{64,80... | collective-permute-start | bytes 221192 | tf_op jit(solution)/shard_map/ppermute | solution.py:316
  3.6 1.6 %collective-permute-start.1 = (f32[6,24,128]{2,1,0:T(8,128)}, f32[6,24,128]{2,1,0:T(8,128)S(1)}, u32[]{:S(2)}, u32[]{:S(2)}) collective-permute-start(f32[6,24,128]{2,1,0:T(8,128)} %shard_map.100.tab), channel_id=1, source_target_pairs={{0,32},{8,40},{16,48},{24,56},{32,0},{40,8},{48,16},{56,24},{64,96... | collective-permute-start | bytes 221192 | tf_op jit(solution)/shard_map/ppermute | solution.py:316
  5.1 1.3 %collective-permute-start.2 = (f32[6,24,128]{2,1,0:T(8,128)}, f32[6,24,128]{2,1,0:T(8,128)S(1)}, u32[]{:S(2)}, u32[]{:S(2)}) collective-permute-start(f32[6,24,128]{2,1,0:T(8,128)} %shard_map.100.tab), channel_id=1, source_target_pairs={{0,48},{8,56},{16,32},{24,40},{32,16},{40,24},{48,0},{56,8},{64,11... | collective-permute-start | bytes 221192 | tf_op jit(solution)/shard_map/ppermute | solution.py:316
  6.4 2.1 %collective-permute-start.4 = (f32[8,128,128]{2,1,0:T(8,128)}, f32[8,128,128]{2,1,0:T(8,128)S(1)}, u32[]{:S(2)}, u32[]{:S(2)}) collective-permute-start(f32[8,128,128]{2,1,0:T(8,128)} %bitcast.14), channel_id=1, source_target_pairs={{0,16},{8,24},{16,0},{24,8},{32,48},{40,56},{48,32},{56,40},{64,80... | collective-permute-start | bytes 1572872 | tf_op jit(solution)/shard_map/ppermute | solution.py:316
  8.6 1.6 %collective-permute-start.5 = (f32[8,128,128]{2,1,0:T(8,128)}, f32[8,128,128]{2,1,0:T(8,128)S(1)}, u32[]{:S(2)}, u32[]{:S(2)}) collective-permute-start(f32[8,128,128]{2,1,0:T(8,128)} %bitcast.15), channel_id=1, source_target_pairs={{0,32},{8,40},{16,48},{24,56},{32,0},{40,8},{48,16},{56,24},{64,96... | collective-permute-start | bytes 1572872 | tf_op jit(solution)/shard_map/ppermute | solution.py:316
  10.9 1.9 %collective-permute-done.2.tabd = f32[6,24,128]{2,1,0:T(8,128)S(1)} collective-permute-done((f32[6,24,128]{2,1,0:T(8,128)}, f32[6,24,128]{2,1,0:T(8,128)S(1)}, u32[]{:S(2)}, u32[]{:S(2)}) %collective-permute-start.2) | collective-permute-done | bytes 73760 | tf_op jit(solution)/shard_map/ppermute | solution.py:316
  12.8 1.2 %collective-permute-start.6 = (f32[8,128,128]{2,1,0:T(8,128)}, f32[8,128,128]{2,1,0:T(8,128)S(1)}, u32[]{:S(2)}, u32[]{:S(2)}) collective-permute-start(f32[8,128,128]{2,1,0:T(8,128)} %bitcast.16), channel_id=1, source_target_pairs={{0,48},{8,56},{16,32},{24,40},{32,16},{40,24},{48,0},{56,8},{64,11... | collective-permute-start | bytes 1572872 | tf_op jit(solution)/shard_map/ppermute | solution.py:316
  15.1 1.2 %copy-done.3 = f32[2,128,1024]{2,1,0:T(8,128)S(1)} copy-done((f32[2,128,1024]{2,1,0:T(8,128)S(1)}, f32[2,128,1024]{2,1,0:T(8,128)}, u32[]{:S(2)}) %copy-start.3) | copy-done | bytes 1048600
  17.0 1.6 %copy-done.5 = bf16[2,8,256,256]{3,2,1,0:T(8,128)(2,1)S(1)} copy-done((bf16[2,8,256,256]{3,2,1,0:T(8,128)(2,1)S(1)}, bf16[2,8,256,256]{3,2,1,0:T(8,128)(2,1)}, u32[]{:S(2)}) %copy-start.5) | copy-done | bytes 2097176
  18.6 16.1 %shard_map.101.cur = bf16[4,8,256,256]{3,2,1,0:T(8,128)(2,1)S(1)} custom-call(s32[4]{0:T(128)S(1)} %pad_add_fusion.bits, f32[2,128,1024]{2,1,0:T(8,128)S(1)} %collective-permute-done.3.other, f32[6,24,128]{2,1,0:T(8,128)S(1)} %copy-done.1, f32[6,24,128]{2,1,0:T(8,128)S(1)} %collective-permute-done.tabx, f32[6,24,128]{2,1,0:T(8,128)S(1)} %collective-permute-done.1.taby, ...), custom_call_target="tpu_custom_call" | custom-call | flops 12000000000 | bytes 1048576 | tf_op jit(solution)/shard_map/pallas_call | solution.py:330
  34.8 2.1 %shard_map.102 = (f32[8,136,256]{2,1,0:T(8,128)S(1)}, f32[8,136,256]{2,1,0:T(8,128)S(1)}) custom-call(s32[32]{0:T(128)S(1)} %maximum_convert_fusion.owners, s32[4]{0:T(128)S(1)} %pad_add_fusion.bits, bf16[4,8,256,256]{3,2,1,0:T(8,128)(2,1)S(1)} %shard_map.101.cur, f32[8,128,128]{2,1,0:T(8,128)S(1)} %bitcast.17, ...), custom_call_target="tpu_custom_call" | custom-call | flops 1000000000 | bytes 1048576 | tf_op jit(solution)/shard_map/pallas_call | solution.py:349
  37.0 2.7 %collective-permute-done.7.taken = f32[8,136,256]{2,1,0:T(8,128)S(1)} collective-permute-done((f32[8,136,256]{2,1,0:T(8,128)S(1)}, f32[8,136,256]{2,1,0:T(8,128)S(1)}, u32[]{:S(2)}, u32[]{:S(2)}) %collective-permute-start.7) | collective-permute-done | bytes 1114144 | tf_op jit(solution)/shard_map/ppermute | solution.py:316
  39.9 3.1 %collective-permute-start.10 = (f32[2,136,256]{2,1,0:T(8,128)S(1)}, f32[2,136,256]{2,1,0:T(8,128)S(1)}, u32[]{:S(2)}, u32[]{:S(2)}) collective-permute-start(f32[2,136,256]{2,1,0:T(8,128)S(1)} %get-tuple-element.25), channel_id=1, source_target_pairs={{0,96},{8,104},{16,112},{24,120},{32,64},{40,72},{48,80},{56,88},{... | collective-permute-start | bytes 835592 | tf_op jit(solution)/shard_map/ppermute | solution.py:316
  43.2 1.5 %collective-permute-start.9 = (f32[2,136,256]{2,1,0:T(8,128)S(1)}, f32[2,136,256]{2,1,0:T(8,128)S(1)}, u32[]{:S(2)}, u32[]{:S(2)}) collective-permute-start(f32[2,136,256]{2,1,0:T(8,128)S(1)} %get-tuple-element.24), channel_id=1, source_target_pairs={{0,64},{8,72},{16,80},{24,88},{32,96},{40,104},{48,112},{56,120},{... | collective-permute-start | bytes 835592 | tf_op jit(solution)/shard_map/ppermute | solution.py:316
  44.7 5.3 %collective-permute-done.10.r3 = f32[2,136,256]{2,1,0:T(8,128)S(1)} collective-permute-done((f32[2,136,256]{2,1,0:T(8,128)S(1)}, f32[2,136,256]{2,1,0:T(8,128)S(1)}, u32[]{:S(2)}, u32[]{:S(2)}) %collective-permute-start.10) | collective-permute-done | bytes 278560 | tf_op jit(solution)/shard_map/ppermute | solution.py:316
  50.0 2.6 %collective-permute-done.8.r1 = f32[2,136,256]{2,1,0:T(8,128)S(1)} collective-permute-done((f32[2,136,256]{2,1,0:T(8,128)S(1)}, f32[2,136,256]{2,1,0:T(8,128)S(1)}, u32[]{:S(2)}, u32[]{:S(2)}) %collective-permute-start.8) | collective-permute-done | bytes 278560 | tf_op jit(solution)/shard_map/ppermute | solution.py:316
  52.6 4.7 %collective-permute-done.9.r2 = f32[2,136,256]{2,1,0:T(8,128)S(1)} collective-permute-done((f32[2,136,256]{2,1,0:T(8,128)S(1)}, f32[2,136,256]{2,1,0:T(8,128)S(1)}, u32[]{:S(2)}, u32[]{:S(2)}) %collective-permute-start.9) | collective-permute-done | bytes 278560 | tf_op jit(solution)/shard_map/ppermute | solution.py:316
  57.3 2.3 %collective-permute-start.11 = (f32[136,256]{1,0:T(8,128)S(1)}, f32[136,256]{1,0:T(8,128)S(1)}, u32[]{:S(2)}, u32[]{:S(2)}) collective-permute-start(f32[136,256]{1,0:T(8,128)S(1)} %get-tuple-element.27), channel_id=1, source_target_pairs={{0,16},{8,24},{16,0},{24,8},{32,48},{40,56},{48,32},{56,40},{64,80... | collective-permute-start | bytes 417800 | tf_op jit(solution)/shard_map/ppermute | solution.py:316
  59.6 4.4 %collective-permute-done.11.taken = f32[136,256]{1,0:T(8,128)S(1)} collective-permute-done((f32[136,256]{1,0:T(8,128)S(1)}, f32[136,256]{1,0:T(8,128)S(1)}, u32[]{:S(2)}, u32[]{:S(2)}) %collective-permute-start.11) | collective-permute-done | bytes 139296 | tf_op jit(solution)/shard_map/ppermute | solution.py:316
  64.1 3.5 %collective-permute-start.12 = (f32[8,256]{1,0:T(8,128)S(1)}, f32[8,256]{1,0:T(8,128)S(1)}, u32[]{:S(2)}, u32[]{:S(2)}) collective-permute-start(f32[8,256]{1,0:T(8,128)S(1)} %get-tuple-element.29), channel_id=1, source_target_pairs={{0,1},{1,2},{2,3},{3,4},{4,5},{5,6},{6,7},{8,9},{9,10},{10,11},{11... | collective-permute-start | bytes 24584 | tf_op jit(solution)/shard_map/ppermute | solution.py:364
  67.6 2.3 %collective-permute-start.13 = (f32[8,256]{1,0:T(8,128)S(1)}, f32[8,256]{1,0:T(8,128)S(1)}, u32[]{:S(2)}, u32[]{:S(2)}) collective-permute-start(f32[8,256]{1,0:T(8,128)S(1)} %get-tuple-element.30), channel_id=1, source_target_pairs={{1,0},{2,1},{3,2},{4,3},{5,4},{6,5},{7,6},{9,8},{10,9},{11,10},{12... | collective-permute-start | bytes 24584 | tf_op jit(solution)/shard_map/ppermute | solution.py:365
  70.6 3.5 %collective-permute-done.13.after = f32[8,256]{1,0:T(8,128)S(1)} collective-permute-done((f32[8,256]{1,0:T(8,128)S(1)}, f32[8,256]{1,0:T(8,128)S(1)}, u32[]{:S(2)}, u32[]{:S(2)}) %collective-permute-start.13) | collective-permute-done | bytes 8224 | tf_op jit(solution)/shard_map/ppermute | solution.py:365
  74.1 2.6 %shard_map.106 = f32[2,128,128]{2,1,0:T(8,128)} custom-call(s32[1,1]{1,0:T(1,128)S(6)} %copy.11.index, f32[16,81]{1,0:T(8,128)S(1)} %copy-done.2, f32[136,256]{1,0:T(8,128)S(1)} %get-tuple-element.28.tile, f32[8,256]{1,0:T(8,128)S(1)} %collective-permute-done.12.before, f32[8,256]{1,0:T(8,128)S(1)} %collective-permute-done.13.after), custom_call_target="tpu_custom_call" | custom-call | flops 1000000 | bytes 1048576 | tf_op jit(solution)/shard_map/pallas_call | solution.py:366
  (29 shorter events, 3.1 us)
Async XLA Ops:
  1.4 8.7 %collective-permute-start = (f32[6,24,128]{2,1,0:T(8,128)}, f32[6,24,128]{2,1,0:T(8,128)S(1)}, u32[]{:S(2)}, u32[]{:S(2)}) collective-permute-start(f32[6,24,128]{2,1,0:T(8,128)} %shard_map.100.tab), channel_id=1, source_target_pairs={{0,16},{8,24},{16,0},{24,8},{32,48},{40,56},{48,32},{56,40},{64,80... | collective-permute-start | bytes 221192 | tf_op jit(solution)/shard_map/ppermute | solution.py:316
  3.6 10.5 %collective-permute-start.1 = (f32[6,24,128]{2,1,0:T(8,128)}, f32[6,24,128]{2,1,0:T(8,128)S(1)}, u32[]{:S(2)}, u32[]{:S(2)}) collective-permute-start(f32[6,24,128]{2,1,0:T(8,128)} %shard_map.100.tab), channel_id=1, source_target_pairs={{0,32},{8,40},{16,48},{24,56},{32,0},{40,8},{48,16},{56,24},{64,96... | collective-permute-start | bytes 221192 | tf_op jit(solution)/shard_map/ppermute | solution.py:316
  5.1 7.7 %collective-permute-start.2 = (f32[6,24,128]{2,1,0:T(8,128)}, f32[6,24,128]{2,1,0:T(8,128)S(1)}, u32[]{:S(2)}, u32[]{:S(2)}) collective-permute-start(f32[6,24,128]{2,1,0:T(8,128)} %shard_map.100.tab), channel_id=1, source_target_pairs={{0,48},{8,56},{16,32},{24,40},{32,16},{40,24},{48,0},{56,8},{64,11... | collective-permute-start | bytes 221192 | tf_op jit(solution)/shard_map/ppermute | solution.py:316
  6.4 28.3 %collective-permute-start.4 = (f32[8,128,128]{2,1,0:T(8,128)}, f32[8,128,128]{2,1,0:T(8,128)S(1)}, u32[]{:S(2)}, u32[]{:S(2)}) collective-permute-start(f32[8,128,128]{2,1,0:T(8,128)} %bitcast.14), channel_id=1, source_target_pairs={{0,16},{8,24},{16,0},{24,8},{32,48},{40,56},{48,32},{56,40},{64,80... | collective-permute-start | bytes 1572872 | tf_op jit(solution)/shard_map/ppermute | solution.py:316
  8.6 26.2 %collective-permute-start.5 = (f32[8,128,128]{2,1,0:T(8,128)}, f32[8,128,128]{2,1,0:T(8,128)S(1)}, u32[]{:S(2)}, u32[]{:S(2)}) collective-permute-start(f32[8,128,128]{2,1,0:T(8,128)} %bitcast.15), channel_id=1, source_target_pairs={{0,32},{8,40},{16,48},{24,56},{32,0},{40,8},{48,16},{56,24},{64,96... | collective-permute-start | bytes 1572872 | tf_op jit(solution)/shard_map/ppermute | solution.py:316
  10.1 4.0 %collective-permute-start.3 = (f32[2,128,1024]{2,1,0:T(8,128)}, f32[2,128,1024]{2,1,0:T(8,128)S(1)}, u32[]{:S(2)}, u32[]{:S(2)}) collective-permute-start(f32[2,128,1024]{2,1,0:T(8,128)} %own_in.1), channel_id=1, source_target_pairs={{0,8},{8,0},{16,24},{24,16},{32,40},{40,32},{48,56},{56,48},{64,72... | collective-permute-start | bytes 3145736 | tf_op jit(solution)/shard_map/ppermute | solution.py:316
  12.8 21.9 %collective-permute-start.6 = (f32[8,128,128]{2,1,0:T(8,128)}, f32[8,128,128]{2,1,0:T(8,128)S(1)}, u32[]{:S(2)}, u32[]{:S(2)}) collective-permute-start(f32[8,128,128]{2,1,0:T(8,128)} %bitcast.16), channel_id=1, source_target_pairs={{0,48},{8,56},{16,32},{24,40},{32,16},{40,24},{48,0},{56,8},{64,11... | collective-permute-start | bytes 1572872 | tf_op jit(solution)/shard_map/ppermute | solution.py:316
  14.1 20.7 %copy-start = (f32[1,1,8,128,128]{4,3,2,1,0:T(8,128)S(1)}, f32[1,1,8,128,128]{4,3,2,1,0:T(8,128)}, u32[]{:S(2)}) copy-start(f32[1,1,8,128,128]{4,3,2,1,0:T(8,128)} %param.16) | copy-start | bytes 1572868
  14.1 0.9 %copy-start.1 = (f32[6,24,128]{2,1,0:T(8,128)S(1)}, f32[6,24,128]{2,1,0:T(8,128)}, u32[]{:S(2)}) copy-start(f32[6,24,128]{2,1,0:T(8,128)} %shard_map.100.tab) | copy-start | bytes 221188
  15.1 1.2 %copy-start.3 = (f32[2,128,1024]{2,1,0:T(8,128)S(1)}, f32[2,128,1024]{2,1,0:T(8,128)}, u32[]{:S(2)}) copy-start(f32[2,128,1024]{2,1,0:T(8,128)} %own_in.1) | copy-start | bytes 3145732
  16.3 0.7 copy-start.4
  17.0 1.6 %copy-start.5 = (bf16[2,8,256,256]{3,2,1,0:T(8,128)(2,1)S(1)}, bf16[2,8,256,256]{3,2,1,0:T(8,128)(2,1)}, u32[]{:S(2)}) copy-start(bf16[2,8,256,256]{3,2,1,0:T(8,128)(2,1)} %constant.12.clone.table_in) | copy-start | bytes 6291460
  36.9 2.8 %collective-permute-start.7 = (f32[8,136,256]{2,1,0:T(8,128)S(1)}, f32[8,136,256]{2,1,0:T(8,128)S(1)}, u32[]{:S(2)}, u32[]{:S(2)}) collective-permute-start(f32[8,136,256]{2,1,0:T(8,128)S(1)} %get-tuple-element.21), channel_id=1, source_target_pairs={{0,8},{8,0},{16,24},{24,16},{32,40},{40,32},{48,56},{56,48},{64,72... | collective-permute-start | bytes 3342344 | tf_op jit(solution)/shard_map/ppermute | solution.py:316
  39.9 34.2 %copy-start.2 = (f32[16,81]{1,0:T(8,128)S(1)}, f32[16,81]{1,0:T(8,128)}, u32[]{:S(2)}) copy-start(f32[16,81]{1,0:T(8,128)} %bank.1) | copy-start | bytes 15556
  39.9 10.1 %collective-permute-start.10 = (f32[2,136,256]{2,1,0:T(8,128)S(1)}, f32[2,136,256]{2,1,0:T(8,128)S(1)}, u32[]{:S(2)}, u32[]{:S(2)}) collective-permute-start(f32[2,136,256]{2,1,0:T(8,128)S(1)} %get-tuple-element.25), channel_id=1, source_target_pairs={{0,96},{8,104},{16,112},{24,120},{32,64},{40,72},{48,80},{56,88},{... | collective-permute-start | bytes 835592 | tf_op jit(solution)/shard_map/ppermute | solution.py:316
  43.0 9.5 %collective-permute-start.8 = (f32[2,136,256]{2,1,0:T(8,128)S(1)}, f32[2,136,256]{2,1,0:T(8,128)S(1)}, u32[]{:S(2)}, u32[]{:S(2)}) collective-permute-start(f32[2,136,256]{2,1,0:T(8,128)S(1)} %get-tuple-element.23), channel_id=1, source_target_pairs={{0,32},{8,40},{16,48},{24,56},{32,0},{40,8},{48,16},{56,24},{64,96... | collective-permute-start | bytes 835592 | tf_op jit(solution)/shard_map/ppermute | solution.py:316
  43.2 14.1 %collective-permute-start.9 = (f32[2,136,256]{2,1,0:T(8,128)S(1)}, f32[2,136,256]{2,1,0:T(8,128)S(1)}, u32[]{:S(2)}, u32[]{:S(2)}) collective-permute-start(f32[2,136,256]{2,1,0:T(8,128)S(1)} %get-tuple-element.24), channel_id=1, source_target_pairs={{0,64},{8,72},{16,80},{24,88},{32,96},{40,104},{48,112},{56,120},{... | collective-permute-start | bytes 835592 | tf_op jit(solution)/shard_map/ppermute | solution.py:316
  57.3 6.6 %collective-permute-start.11 = (f32[136,256]{1,0:T(8,128)S(1)}, f32[136,256]{1,0:T(8,128)S(1)}, u32[]{:S(2)}, u32[]{:S(2)}) collective-permute-start(f32[136,256]{1,0:T(8,128)S(1)} %get-tuple-element.27), channel_id=1, source_target_pairs={{0,16},{8,24},{16,0},{24,8},{32,48},{40,56},{48,32},{56,40},{64,80... | collective-permute-start | bytes 417800 | tf_op jit(solution)/shard_map/ppermute | solution.py:316
  64.1 6.5 %collective-permute-start.12 = (f32[8,256]{1,0:T(8,128)S(1)}, f32[8,256]{1,0:T(8,128)S(1)}, u32[]{:S(2)}, u32[]{:S(2)}) collective-permute-start(f32[8,256]{1,0:T(8,128)S(1)} %get-tuple-element.29), channel_id=1, source_target_pairs={{0,1},{1,2},{2,3},{3,4},{4,5},{5,6},{6,7},{8,9},{9,10},{10,11},{11... | collective-permute-start | bytes 24584 | tf_op jit(solution)/shard_map/ppermute | solution.py:364
  67.6 6.4 %collective-permute-start.13 = (f32[8,256]{1,0:T(8,128)S(1)}, f32[8,256]{1,0:T(8,128)S(1)}, u32[]{:S(2)}, u32[]{:S(2)}) collective-permute-start(f32[8,256]{1,0:T(8,128)S(1)} %get-tuple-element.30), channel_id=1, source_target_pairs={{1,0},{2,1},{3,2},{4,3},{5,4},{6,5},{7,6},{9,8},{10,9},{11,10},{12... | collective-permute-start | bytes 24584 | tf_op jit(solution)/shard_map/ppermute | solution.py:365

commit v4 on v3

--- a/solution.py
+++ b/solution.py
@@ -160,16 +160,16 @@
 
 def gained(blocks, gain, section):
     re, im = blocks
-    rows = [gain[section : section + 1, A * k : A * k + A] * F32(1.0 / N) for k in range(8)]
+    rows = [gain[6, 8 * section + k : 8 * section + k + 1, :] for k in range(8)]
     return [v * g for v, g in zip(re, rows)], [v * g for v, g in zip(im, rows)]
 
 
 def merge_kernel(
-    bits, other, tab, tabx, taby, tabd, own_in, gain_in, table_in, out, zz, uu, mats, phases, steps, own, gain, table, sems
+    bits, other, tab, tabx, taby, tabd, own_in, table_in, out, zz, uu, mats, phases, steps, own, table, sems
 ):
     copies = [
         pltpu.make_async_copy(source, target, sems.at[k])
-        for k, (source, target) in enumerate(((own_in, own), (table_in, table), (gain_in, gain)))
+        for k, (source, target) in enumerate(((own_in, own), (table_in, table)))
     ]
     for copy in copies:
         copy.start()
@@ -188,12 +188,12 @@
     for copy in copies:
         copy.wait()
     first = run([blocks(own), blocks(other)], [[(0, 0), (1, 1)]])
-    y = gained(first[0], gain, 0)
+    y = gained(first[0], tab, 0)
     second = run([y], [[(0, 2)], [(0, 3)]])
-    z = [gained(v, gain, 1) for v in second]
+    z = [gained(v, tab, 1) for v in second]
     third = run(z, [[(0, 4)], [(1, 5)], [(0, 6)], [(1, 7)]])
     for j, v in enumerate(third):
-        re, im = gained(v, gain, 2)
+        re, im = gained(v, tab, 2)
         for q in range(8):
             h, l = split(jnp.concatenate([re[q], im[q]], axis=1))
             out[j, q, 0:A] = h
@@ -238,7 +238,7 @@
         ref[...] = (g0[k] + r1[k]) + (r2[k] + r3[k])
 
 
-def table_kernel(owners, index, weight, shift, out):
+def table_kernel(owners, index, weight, shift, gain, out):
     lane = lax.broadcasted_iota(jnp.int32, (4, A), 1)
     row = jnp.zeros((4, A), jnp.int32)
     for q in range(8):
@@ -249,6 +249,10 @@
         out[k, 8:16] = weight[section, 0, child]
         out[k, 16:20] = jnp.broadcast_to(shift[section, 0, child : child + 1, :], (4, A))
         out[k, 20:24] = row.astype(F32)
+    for section in range(3):
+        for k in range(8):
+            at = 8 * section + k
+            out[6, at : at + 1] = gain[section : section + 1, A * k : A * k + A] * F32(1.0 / N)
 
 
 def tile_kernel(mine, taken, tile, first, last):
@@ -265,35 +269,59 @@
         ref[:, A:] = ends.T[:8]
 
 
-def filter_kernel(index, bank, tile, before, after, out, pad, moved):
+def filter_kernel(index, bank, tile, out, pad, moved, lines):
     number = index[0, 0]
-    sides = []
-    for ref in (before, after):
-        blank = jnp.zeros((A - 8, A), F32)
-        main = jnp.concatenate([ref[:, :A], blank], axis=0).T
-        ends = jnp.concatenate([ref[:, A:], blank], axis=0).T
-        sides.append(jnp.concatenate([main, ends[:8]], axis=0))
     lane = lax.broadcasted_iota(jnp.int32, (ROWS, A), 1)
     for p in range(2):
         body = tile[:, A * p : A * p + A]
         turned = pltpu.roll(body, 4, 1)
-        lead = sides[0] if p == 0 else pltpu.roll(sides[0], A - 4, 1)
-        tail = pltpu.roll(sides[1], 4, 1) if p == 0 else sides[1]
-        left = jnp.where(lane < 4, lead, turned)
-        right = jnp.where(lane < 4, turned, tail)
+        left = jnp.where(lane < 4, 0.0, turned)
+        right = jnp.where(lane < 4, turned, 0.0)
         for half, value in enumerate((left, right)):
             pad[4 : 4 + A, A * half : A * half + A] = value[0:A]
             pad[0:4, A * half : A * half + A] = value[A : A + 4]
             pad[A + 4 :, A * half : A * half + A] = value[A + 4 :]
+        for v in range(9):
+            moved[v] = pltpu.roll(pad[...], H - v, 1)[:, :A] if v else pad[:, :A]
         total = jnp.zeros((A, A), F32)
-        for v in range(9):
-            if v:
-                moved[...] = pltpu.roll(pad[...], H - v, 1)[:, :A]
+        for u in range(9):
+            line = bank[number, 9 * u] * moved[0]
+            for v in range(1, 9):
+                line = line + bank[number, 9 * u + v] * moved[v]
+            lines[p, u] = line
+            total = total + lines[p, u, u : u + A, :]
+        out[p] = total
+
+
+def side_kernel(index, bank, main, before, after, out):
+    number = index[0, 0]
+    lane = lax.broadcasted_iota(jnp.int32, (8, H), 1)
+    row = lax.broadcasted_iota(jnp.int32, (8, A), 0)
+    sums = []
+    for ref, first in ((before, 0), (after, 5)):
+        value = ref[...]
+        ends = pltpu.roll(value, A, 1)
+        spread = jnp.where(lane < 4, ends, jnp.where(lane < A + 4, pltpu.roll(value, 4, 1), value))
+        turned = [pltpu.roll(spread, H - u, 1)[:, :A] if u else spread[:, :A] for u in range(9)]
+        total = jnp.zeros((8, A), F32)
+        for v in range(first, first + 4):
+            line = bank[number, v] * turned[0]
+            for u in range(1, 9):
+                line = line + bank[number, 9 * u + v] * turned[u]
+            if first == 0:
+                line = pltpu.roll(line, 8 - v, 0) if v else line
+                total = total + jnp.where(row % 4 + v < 4, line, 0.0)
             else:
-                moved[...] = pad[:, :A]
-            for u in range(9):
-                total = total + bank[number, 9 * u + v] * moved[u : u + A, :]
-        out[p] = total
+                line = pltpu.roll(line, 8 - v, 0) if v < 8 else line
+                total = total + jnp.where(row % 4 >= 8 - v, line, 0.0)
+        sums.append(total)
+    blank = jnp.zeros((A - 16, A), F32)
+    for p in range(2):
+        head = sums[0] if p == 0 else pltpu.roll(sums[0], 4, 0)
+        tail = sums[1] if p == 1 else pltpu.roll(sums[1], 4, 0)
+        head = jnp.where(row < 4, head, 0.0)
+        tail = jnp.where(row >= 4, tail, 0.0)
+        out[p] = main[p] + jnp.concatenate([head, blank, tail], axis=0).T
 
 
 def call(kernel, out_shape, in_specs, scratch=(), flops=1000000, limit=16):
@@ -321,8 +349,8 @@
     bits = jnp.stack([place & 1, (place >> 1) & 1, (place >> 2) & 1, place])
     own_weights = weights[0, 0]
     wx, wy, wd = (swap(own_weights, mask) for mask in (2, 4, 6))
-    tab = call(table_kernel, struct((6, 24, A)), [SMEM] + [VMEM] * 3, limit=60)(
-        tile_owner.reshape(8), tap_index, tap_weight, range_shift
+    tab = call(table_kernel, struct((7, 24, A)), [SMEM] + [VMEM] * 4, limit=60)(
+        tile_owner.reshape(8), tap_index, tap_weight, range_shift, range_gain
     )
     tabx, taby, tabd = (swap(tab, mask) for mask in (2, 4, 6))
     tabx, late = lax.optimization_barrier((tabx, polar))
@@ -330,7 +358,7 @@
     cur = call(
         merge_kernel,
         struct((4, 8, 2 * A, H), BF16),
-        [SMEM] + [VMEM] * 5 + [HBM] * 3,
+        [SMEM] + [VMEM] * 5 + [HBM] * 2,
         [
             pltpu.VMEM((8, 4 * A, H), BF16),
             pltpu.VMEM((8, 4 * A, H), F32),
@@ -338,13 +366,12 @@
             pltpu.VMEM((8, 2, A, A), F32),
             pltpu.VMEM((8, 2, A, A), F32),
             pltpu.VMEM((2, A, N), F32),
-            pltpu.VMEM((3, N), F32),
             pltpu.VMEM((2, 8, H, H), BF16),
-            pltpu.SemaphoreType.DMA((3,)),
+            pltpu.SemaphoreType.DMA((2,)),
         ],
         flops=12 * 10**9,
         limit=32,
-    )(bits, other, tab, tabx, taby, tabd, polar, range_gain, jnp.asarray(dft_tables()))
+    )(bits, other, tab, tabx, taby, tabd, polar, jnp.asarray(dft_tables()))
     owners = jnp.concatenate([t[0, 20, 0:8] for t in (tab, tabx, taby, tabd)]).astype(jnp.int32)
     keep, send = call(
         contrib_kernel,
@@ -363,12 +390,18 @@
     )(mine, taken)
     before = lax.ppermute(last, "swath", [(i, i + 1) for i in range(7)])
     after = lax.ppermute(first, "swath", [(i + 1, i) for i in range(7)])
-    return call(
+    main = call(
         filter_kernel,
         struct((2, A, A)),
-        [SMEM, SMEM] + [VMEM] * 3,
-        [pltpu.VMEM((ROWS, H), F32), pltpu.VMEM((ROWS, A), F32)],
-    )(kernel_index, bank, tile, before, after)
+        [SMEM, SMEM, VMEM],
+        [
+            pltpu.VMEM((ROWS, H), F32),
+            pltpu.VMEM((9, ROWS, A), F32),
+            pltpu.VMEM((2, 9, ROWS, A), F32),
+        ],
+        flops=10**9,
+    )(kernel_index, bank, tile)
+    return call(side_kernel, struct((2, A, A)), [SMEM, SMEM] + [VMEM] * 3)(kernel_index, bank, main, before, after)
 
 
 def solution(mesh):

time: 77.9 us -> 76.3 us (0.979)
  waiting for transfers between devices: 25 us -> 23.8 us
  Pallas kernels: 22.7 us -> 23.5 us
    ppermute x1, waiting for transfers between devices: 3.47 us -> 2.65 us  [shards(): after = lax.ppermute(first, 'swath', [(i + 1, i) for i in range(7)])]
    pallas_call x2 -> x3, Pallas kernels: 4.08 us -> 4.88 us  [the longest x1 1.84 us: shards(): call(filter_kernel, struct((2, A, A)), [SMEM, SMEM, VMEM], [pltpu.VMEM((R...]
    unnamed x12 -> x10, local copies, waits for them, and re-layouts: 4.48 us -> 3.77 us
  transfers between devices with their start and end apart: 14 -> 14, of which waited for: 7 -> 7; matrix products, arithmetic and copies ran while one was open for 1% -> 1% of each run, Pallas kernels for 21% -> 24%
where the time goes in v4:
time: 76.3 us; the launch traced here: 75.8 us
  waiting for transfers between devices  23.8 us (31%)
  Pallas kernels  23.5 us (31%)
  starting transfers between devices  23.1 us (30%)
  local copies, waits for them, and re-layouts  4.47 us (6%)
  between operations  0.78 us (1%)
    ppermute x12, waiting for transfers between devices, swap(): return lax.ppermute(value, 'aper', [(i, i ^ mask) for i in range(16)])  21.1 us
    ppermute x12, starting transfers between devices, swap(): return lax.ppermute(value, 'aper', [(i, i ^ mask) for i in range(16)])  17.1 us
    pallas_call x1, Pallas kernels, shards(): call(merge_kernel, struct((4, 8, 2 * A, H), BF16), [SMEM] + [VMEM] * 5 +...  16.1 us
    ppermute x1, starting transfers between devices, shards(): before = lax.ppermute(last, 'swath', [(i, i + 1) for i in range(7)])  4.14 us
    unnamed x10, local copies, waits for them, and re-layouts  3.77 us
    ppermute x1, waiting for transfers between devices, shards(): after = lax.ppermute(first, 'swath', [(i + 1, i) for i in range(7)])  2.65 us
    pallas_call x1, Pallas kernels, shards(): call(contrib_kernel, (struct((8, ROWS, H)), struct((8, ROWS, H))), [SMEM,...  2.16 us
    ppermute x1, starting transfers between devices, shards(): after = lax.ppermute(first, 'swath', [(i + 1, i) for i in range(7)])  1.92 us
  transfers between devices with their start and end apart: 14, of which 7 were waited for; matrix products, arithmetic and copies ran while one was open for 1% of the time, Pallas kernels for 24%

profile of v4, /device:TPU:34, one launch (start us, length us, event | category | flops | bytes accessed | tf_op | source)
XLA Modules:
  0.0 75.8 jit_solution(15390396589301358563)
XLA Ops:
  0.0 1.5 %shard_map.100.tab = f32[7,24,128]{2,1,0:T(8,128)} custom-call(s32[8]{0:T(128)} %bitcast.18, s32[3,1,2,8,128]{4,3,2,1,0:T(8,128)} %index.3, f32[3,1,2,8,128]{4,3,2,1,0:T(8,128)} %weight.1, f32[3,1,2,128]{3,2,1,0:T(2,128)} %shift.1, f32[3,1024]{1,0:T(4,128)} %gain.1), custom_call_target="tpu_custom_call" | custom-call | flops 1000000 | bytes 1048576 | tf_op jit(solution)/shard_map/pallas_call | solution.py:352
  1.5 2.1 %collective-permute-start = (f32[7,24,128]{2,1,0:T(8,128)}, f32[7,24,128]{2,1,0:T(8,128)S(1)}, u32[]{:S(2)}, u32[]{:S(2)}) collective-permute-start(f32[7,24,128]{2,1,0:T(8,128)} %shard_map.100.tab), channel_id=1, source_target_pairs={{0,16},{8,24},{16,0},{24,8},{32,48},{40,56},{48,32},{56,40},{64,80... | collective-permute-start | bytes 258056 | tf_op jit(solution)/shard_map/ppermute | solution.py:344
  3.6 1.6 %collective-permute-start.1 = (f32[7,24,128]{2,1,0:T(8,128)}, f32[7,24,128]{2,1,0:T(8,128)S(1)}, u32[]{:S(2)}, u32[]{:S(2)}) collective-permute-start(f32[7,24,128]{2,1,0:T(8,128)} %shard_map.100.tab), channel_id=1, source_target_pairs={{0,32},{8,40},{16,48},{24,56},{32,0},{40,8},{48,16},{56,24},{64,96... | collective-permute-start | bytes 258056 | tf_op jit(solution)/shard_map/ppermute | solution.py:344
  5.2 1.3 %collective-permute-start.2 = (f32[7,24,128]{2,1,0:T(8,128)}, f32[7,24,128]{2,1,0:T(8,128)S(1)}, u32[]{:S(2)}, u32[]{:S(2)}) collective-permute-start(f32[7,24,128]{2,1,0:T(8,128)} %shard_map.100.tab), channel_id=1, source_target_pairs={{0,48},{8,56},{16,32},{24,40},{32,16},{40,24},{48,0},{56,8},{64,11... | collective-permute-start | bytes 258056 | tf_op jit(solution)/shard_map/ppermute | solution.py:344
  6.5 2.1 %collective-permute-start.4 = (f32[8,128,128]{2,1,0:T(8,128)}, f32[8,128,128]{2,1,0:T(8,128)S(1)}, u32[]{:S(2)}, u32[]{:S(2)}) collective-permute-start(f32[8,128,128]{2,1,0:T(8,128)} %bitcast.14), channel_id=1, source_target_pairs={{0,16},{8,24},{16,0},{24,8},{32,48},{40,56},{48,32},{56,40},{64,80... | collective-permute-start | bytes 1572872 | tf_op jit(solution)/shard_map/ppermute | solution.py:344
  8.6 1.6 %collective-permute-start.5 = (f32[8,128,128]{2,1,0:T(8,128)}, f32[8,128,128]{2,1,0:T(8,128)S(1)}, u32[]{:S(2)}, u32[]{:S(2)}) collective-permute-start(f32[8,128,128]{2,1,0:T(8,128)} %bitcast.15), channel_id=1, source_target_pairs={{0,32},{8,40},{16,48},{24,56},{32,0},{40,8},{48,16},{56,24},{64,96... | collective-permute-start | bytes 1572872 | tf_op jit(solution)/shard_map/ppermute | solution.py:344
  10.9 2.2 %collective-permute-done.2.tabd = f32[7,24,128]{2,1,0:T(8,128)S(1)} collective-permute-done((f32[7,24,128]{2,1,0:T(8,128)}, f32[7,24,128]{2,1,0:T(8,128)S(1)}, u32[]{:S(2)}, u32[]{:S(2)}) %collective-permute-start.2) | collective-permute-done | bytes 86048 | tf_op jit(solution)/shard_map/ppermute | solution.py:344
  15.4 1.2 %copy-done.3 = f32[2,128,1024]{2,1,0:T(8,128)S(1)} copy-done((f32[2,128,1024]{2,1,0:T(8,128)S(1)}, f32[2,128,1024]{2,1,0:T(8,128)}, u32[]{:S(2)}) %copy-start.3) | copy-done | bytes 1048600
  16.6 1.6 %copy-done.4 = bf16[2,8,256,256]{3,2,1,0:T(8,128)(2,1)S(1)} copy-done((bf16[2,8,256,256]{3,2,1,0:T(8,128)(2,1)S(1)}, bf16[2,8,256,256]{3,2,1,0:T(8,128)(2,1)}, u32[]{:S(2)}) %copy-start.4) | copy-done | bytes 2097176
  18.2 16.1 %shard_map.101.cur = bf16[4,8,256,256]{3,2,1,0:T(8,128)(2,1)S(1)} custom-call(s32[4]{0:T(128)S(1)} %pad_add_fusion.bits, f32[2,128,1024]{2,1,0:T(8,128)S(1)} %collective-permute-done.3.other, f32[7,24,128]{2,1,0:T(8,128)S(1)} %copy-done.1, f32[7,24,128]{2,1,0:T(8,128)S(1)} %collective-permute-done.tabx, f32[7,24,128]{2,1,0:T(8,128)S(1)} %collective-permute-done.1.taby, ...), custom_call_target="tpu_custom_call" | custom-call | flops 12000000000 | bytes 1048576 | tf_op jit(solution)/shard_map/pallas_call | solution.py:358
  34.4 2.2 %shard_map.102 = (f32[8,136,256]{2,1,0:T(8,128)S(1)}, f32[8,136,256]{2,1,0:T(8,128)S(1)}) custom-call(s32[32]{0:T(128)S(1)} %maximum_convert_fusion.owners, s32[4]{0:T(128)S(1)} %pad_add_fusion.bits, bf16[4,8,256,256]{3,2,1,0:T(8,128)(2,1)S(1)} %shard_map.101.cur, f32[8,128,128]{2,1,0:T(8,128)S(1)} %bitcast.17, ...), custom_call_target="tpu_custom_call" | custom-call | flops 1000000000 | bytes 1048576 | tf_op jit(solution)/shard_map/pallas_call | solution.py:376
  36.6 2.7 %collective-permute-done.7.taken = f32[8,136,256]{2,1,0:T(8,128)S(1)} collective-permute-done((f32[8,136,256]{2,1,0:T(8,128)S(1)}, f32[8,136,256]{2,1,0:T(8,128)S(1)}, u32[]{:S(2)}, u32[]{:S(2)}) %collective-permute-start.7) | collective-permute-done | bytes 1114144 | tf_op jit(solution)/shard_map/ppermute | solution.py:344
  39.5 3.1 %collective-permute-start.10 = (f32[2,136,256]{2,1,0:T(8,128)S(1)}, f32[2,136,256]{2,1,0:T(8,128)S(1)}, u32[]{:S(2)}, u32[]{:S(2)}) collective-permute-start(f32[2,136,256]{2,1,0:T(8,128)S(1)} %get-tuple-element.25), channel_id=1, source_target_pairs={{0,96},{8,104},{16,112},{24,120},{32,64},{40,72},{48,80},{56,88},{... | collective-permute-start | bytes 835592 | tf_op jit(solution)/shard_map/ppermute | solution.py:344
  42.7 1.5 %collective-permute-start.9 = (f32[2,136,256]{2,1,0:T(8,128)S(1)}, f32[2,136,256]{2,1,0:T(8,128)S(1)}, u32[]{:S(2)}, u32[]{:S(2)}) collective-permute-start(f32[2,136,256]{2,1,0:T(8,128)S(1)} %get-tuple-element.24), channel_id=1, source_target_pairs={{0,64},{8,72},{16,80},{24,88},{32,96},{40,104},{48,112},{56,120},{... | collective-permute-start | bytes 835592 | tf_op jit(solution)/shard_map/ppermute | solution.py:344
  44.3 5.3 %collective-permute-done.10.r3 = f32[2,136,256]{2,1,0:T(8,128)S(1)} collective-permute-done((f32[2,136,256]{2,1,0:T(8,128)S(1)}, f32[2,136,256]{2,1,0:T(8,128)S(1)}, u32[]{:S(2)}, u32[]{:S(2)}) %collective-permute-start.10) | collective-permute-done | bytes 278560 | tf_op jit(solution)/shard_map/ppermute | solution.py:344
  49.5 2.6 %collective-permute-done.8.r1 = f32[2,136,256]{2,1,0:T(8,128)S(1)} collective-permute-done((f32[2,136,256]{2,1,0:T(8,128)S(1)}, f32[2,136,256]{2,1,0:T(8,128)S(1)}, u32[]{:S(2)}, u32[]{:S(2)}) %collective-permute-start.8) | collective-permute-done | bytes 278560 | tf_op jit(solution)/shard_map/ppermute | solution.py:344
  52.1 4.7 %collective-permute-done.9.r2 = f32[2,136,256]{2,1,0:T(8,128)S(1)} collective-permute-done((f32[2,136,256]{2,1,0:T(8,128)S(1)}, f32[2,136,256]{2,1,0:T(8,128)S(1)}, u32[]{:S(2)}, u32[]{:S(2)}) %collective-permute-start.9) | collective-permute-done | bytes 278560 | tf_op jit(solution)/shard_map/ppermute | solution.py:344
  56.8 2.3 %collective-permute-start.11 = (f32[136,256]{1,0:T(8,128)S(1)}, f32[136,256]{1,0:T(8,128)S(1)}, u32[]{:S(2)}, u32[]{:S(2)}) collective-permute-start(f32[136,256]{1,0:T(8,128)S(1)} %get-tuple-element.27), channel_id=1, source_target_pairs={{0,16},{8,24},{16,0},{24,8},{32,48},{40,56},{48,32},{56,40},{64,80... | collective-permute-start | bytes 417800 | tf_op jit(solution)/shard_map/ppermute | solution.py:344
  59.8 3.7 %collective-permute-done.11.taken = f32[136,256]{1,0:T(8,128)S(1)} collective-permute-done((f32[136,256]{1,0:T(8,128)S(1)}, f32[136,256]{1,0:T(8,128)S(1)}, u32[]{:S(2)}, u32[]{:S(2)}) %collective-permute-start.11) | collective-permute-done | bytes 139296 | tf_op jit(solution)/shard_map/ppermute | solution.py:344
  63.7 4.1 %collective-permute-start.12 = (f32[8,256]{1,0:T(8,128)S(1)}, f32[8,256]{1,0:T(8,128)S(1)}, u32[]{:S(2)}, u32[]{:S(2)}) collective-permute-start(f32[8,256]{1,0:T(8,128)S(1)} %get-tuple-element.29), channel_id=1, source_target_pairs={{0,1},{1,2},{2,3},{3,4},{4,5},{5,6},{6,7},{8,9},{9,10},{10,11},{11... | collective-permute-start | bytes 24584 | tf_op jit(solution)/shard_map/ppermute | solution.py:391
  67.8 1.9 %collective-permute-start.13 = (f32[8,256]{1,0:T(8,128)S(1)}, f32[8,256]{1,0:T(8,128)S(1)}, u32[]{:S(2)}, u32[]{:S(2)}) collective-permute-start(f32[8,256]{1,0:T(8,128)S(1)} %get-tuple-element.30), channel_id=1, source_target_pairs={{1,0},{2,1},{3,2},{4,3},{5,4},{6,5},{7,6},{9,8},{10,9},{11,10},{12... | collective-permute-start | bytes 24584 | tf_op jit(solution)/shard_map/ppermute | solution.py:392
  69.8 1.8 %shard_map.106.main = f32[2,128,128]{2,1,0:T(8,128)S(1)} custom-call(s32[1,1]{1,0:T(1,128)S(6)} %copy.11.index, f32[16,81]{1,0:T(8,128)S(1)} %copy-done.2, f32[136,256]{1,0:T(8,128)S(1)} %get-tuple-element.28.tile), custom_call_target="tpu_custom_call" | custom-call | flops 1000000000 | bytes 1048576 | tf_op jit(solution)/shard_map/pallas_call | solution.py:393
  71.6 2.6 %collective-permute-done.13.after = f32[8,256]{1,0:T(8,128)S(1)} collective-permute-done((f32[8,256]{1,0:T(8,128)S(1)}, f32[8,256]{1,0:T(8,128)S(1)}, u32[]{:S(2)}, u32[]{:S(2)}) %collective-permute-start.13) | collective-permute-done | bytes 8224 | tf_op jit(solution)/shard_map/ppermute | solution.py:392
  74.3 1.6 %shard_map.107 = f32[2,128,128]{2,1,0:T(8,128)} custom-call(s32[1,1]{1,0:T(1,128)S(6)} %copy.11.index, f32[16,81]{1,0:T(8,128)S(1)} %copy-done.2, f32[2,128,128]{2,1,0:T(8,128)S(1)} %shard_map.106.main, f32[8,256]{1,0:T(8,128)S(1)} %collective-permute-done.12.before, f32[8,256]{1,0:T(8,128)S(1)} %collective-permute-done.13.after), custom_call_target="tpu_custom_call" | custom-call | flops 1000000 | bytes 1048576 | tf_op jit(solution)/shard_map/pallas_call | solution.py:404
  (28 shorter events, 3.6 us)
Async XLA Ops:
  1.5 8.7 %collective-permute-start = (f32[7,24,128]{2,1,0:T(8,128)}, f32[7,24,128]{2,1,0:T(8,128)S(1)}, u32[]{:S(2)}, u32[]{:S(2)}) collective-permute-start(f32[7,24,128]{2,1,0:T(8,128)} %shard_map.100.tab), channel_id=1, source_target_pairs={{0,16},{8,24},{16,0},{24,8},{32,48},{40,56},{48,32},{56,40},{64,80... | collective-permute-start | bytes 258056 | tf_op jit(solution)/shard_map/ppermute | solution.py:344
  3.6 10.7 %collective-permute-start.1 = (f32[7,24,128]{2,1,0:T(8,128)}, f32[7,24,128]{2,1,0:T(8,128)S(1)}, u32[]{:S(2)}, u32[]{:S(2)}) collective-permute-start(f32[7,24,128]{2,1,0:T(8,128)} %shard_map.100.tab), channel_id=1, source_target_pairs={{0,32},{8,40},{16,48},{24,56},{32,0},{40,8},{48,16},{56,24},{64,96... | collective-permute-start | bytes 258056 | tf_op jit(solution)/shard_map/ppermute | solution.py:344
  5.2 8.0 %collective-permute-start.2 = (f32[7,24,128]{2,1,0:T(8,128)}, f32[7,24,128]{2,1,0:T(8,128)S(1)}, u32[]{:S(2)}, u32[]{:S(2)}) collective-permute-start(f32[7,24,128]{2,1,0:T(8,128)} %shard_map.100.tab), channel_id=1, source_target_pairs={{0,48},{8,56},{16,32},{24,40},{32,16},{40,24},{48,0},{56,8},{64,11... | collective-permute-start | bytes 258056 | tf_op jit(solution)/shard_map/ppermute | solution.py:344
  6.5 27.9 %collective-permute-start.4 = (f32[8,128,128]{2,1,0:T(8,128)}, f32[8,128,128]{2,1,0:T(8,128)S(1)}, u32[]{:S(2)}, u32[]{:S(2)}) collective-permute-start(f32[8,128,128]{2,1,0:T(8,128)} %bitcast.14), channel_id=1, source_target_pairs={{0,16},{8,24},{16,0},{24,8},{32,48},{40,56},{48,32},{56,40},{64,80... | collective-permute-start | bytes 1572872 | tf_op jit(solution)/shard_map/ppermute | solution.py:344
  8.6 25.8 %collective-permute-start.5 = (f32[8,128,128]{2,1,0:T(8,128)}, f32[8,128,128]{2,1,0:T(8,128)S(1)}, u32[]{:S(2)}, u32[]{:S(2)}) collective-permute-start(f32[8,128,128]{2,1,0:T(8,128)} %bitcast.15), channel_id=1, source_target_pairs={{0,32},{8,40},{16,48},{24,56},{32,0},{40,8},{48,16},{56,24},{64,96... | collective-permute-start | bytes 1572872 | tf_op jit(solution)/shard_map/ppermute | solution.py:344
  10.2 4.3 %collective-permute-start.3 = (f32[2,128,1024]{2,1,0:T(8,128)}, f32[2,128,1024]{2,1,0:T(8,128)S(1)}, u32[]{:S(2)}, u32[]{:S(2)}) collective-permute-start(f32[2,128,1024]{2,1,0:T(8,128)} %own_in.1), channel_id=1, source_target_pairs={{0,8},{8,0},{16,24},{24,16},{32,40},{40,32},{48,56},{56,48},{64,72... | collective-permute-start | bytes 3145736 | tf_op jit(solution)/shard_map/ppermute | solution.py:344
  13.1 21.2 %collective-permute-start.6 = (f32[8,128,128]{2,1,0:T(8,128)}, f32[8,128,128]{2,1,0:T(8,128)S(1)}, u32[]{:S(2)}, u32[]{:S(2)}) collective-permute-start(f32[8,128,128]{2,1,0:T(8,128)} %bitcast.16), channel_id=1, source_target_pairs={{0,48},{8,56},{16,32},{24,40},{32,16},{40,24},{48,0},{56,8},{64,11... | collective-permute-start | bytes 1572872 | tf_op jit(solution)/shard_map/ppermute | solution.py:344
  14.4 19.9 %copy-start = (f32[1,1,8,128,128]{4,3,2,1,0:T(8,128)S(1)}, f32[1,1,8,128,128]{4,3,2,1,0:T(8,128)}, u32[]{:S(2)}) copy-start(f32[1,1,8,128,128]{4,3,2,1,0:T(8,128)} %param.16) | copy-start | bytes 1572868
  14.4 0.9 %copy-start.1 = (f32[7,24,128]{2,1,0:T(8,128)S(1)}, f32[7,24,128]{2,1,0:T(8,128)}, u32[]{:S(2)}) copy-start(f32[7,24,128]{2,1,0:T(8,128)} %shard_map.100.tab) | copy-start | bytes 258052
  15.4 1.2 %copy-start.3 = (f32[2,128,1024]{2,1,0:T(8,128)S(1)}, f32[2,128,1024]{2,1,0:T(8,128)}, u32[]{:S(2)}) copy-start(f32[2,128,1024]{2,1,0:T(8,128)} %own_in.1) | copy-start | bytes 3145732
  16.6 1.6 %copy-start.4 = (bf16[2,8,256,256]{3,2,1,0:T(8,128)(2,1)S(1)}, bf16[2,8,256,256]{3,2,1,0:T(8,128)(2,1)}, u32[]{:S(2)}) copy-start(bf16[2,8,256,256]{3,2,1,0:T(8,128)(2,1)} %constant.12.clone.table_in) | copy-start | bytes 6291460
  36.5 2.8 %collective-permute-start.7 = (f32[8,136,256]{2,1,0:T(8,128)S(1)}, f32[8,136,256]{2,1,0:T(8,128)S(1)}, u32[]{:S(2)}, u32[]{:S(2)}) collective-permute-start(f32[8,136,256]{2,1,0:T(8,128)S(1)} %get-tuple-element.21), channel_id=1, source_target_pairs={{0,8},{8,0},{16,24},{24,16},{32,40},{40,32},{48,56},{56,48},{64,72... | collective-permute-start | bytes 3342344 | tf_op jit(solution)/shard_map/ppermute | solution.py:344
  39.5 30.3 %copy-start.2 = (f32[16,81]{1,0:T(8,128)S(1)}, f32[16,81]{1,0:T(8,128)}, u32[]{:S(2)}) copy-start(f32[16,81]{1,0:T(8,128)} %bank.3) | copy-start | bytes 15556
  39.5 10.0 %collective-permute-start.10 = (f32[2,136,256]{2,1,0:T(8,128)S(1)}, f32[2,136,256]{2,1,0:T(8,128)S(1)}, u32[]{:S(2)}, u32[]{:S(2)}) collective-permute-start(f32[2,136,256]{2,1,0:T(8,128)S(1)} %get-tuple-element.25), channel_id=1, source_target_pairs={{0,96},{8,104},{16,112},{24,120},{32,64},{40,72},{48,80},{56,88},{... | collective-permute-start | bytes 835592 | tf_op jit(solution)/shard_map/ppermute | solution.py:344
  42.6 9.5 %collective-permute-start.8 = (f32[2,136,256]{2,1,0:T(8,128)S(1)}, f32[2,136,256]{2,1,0:T(8,128)S(1)}, u32[]{:S(2)}, u32[]{:S(2)}) collective-permute-start(f32[2,136,256]{2,1,0:T(8,128)S(1)} %get-tuple-element.23), channel_id=1, source_target_pairs={{0,32},{8,40},{16,48},{24,56},{32,0},{40,8},{48,16},{56,24},{64,96... | collective-permute-start | bytes 835592 | tf_op jit(solution)/shard_map/ppermute | solution.py:344
  42.7 14.0 %collective-permute-start.9 = (f32[2,136,256]{2,1,0:T(8,128)S(1)}, f32[2,136,256]{2,1,0:T(8,128)S(1)}, u32[]{:S(2)}, u32[]{:S(2)}) collective-permute-start(f32[2,136,256]{2,1,0:T(8,128)S(1)} %get-tuple-element.24), channel_id=1, source_target_pairs={{0,64},{8,72},{16,80},{24,88},{32,96},{40,104},{48,112},{56,120},{... | collective-permute-start | bytes 835592 | tf_op jit(solution)/shard_map/ppermute | solution.py:344
  56.8 6.6 %collective-permute-start.11 = (f32[136,256]{1,0:T(8,128)S(1)}, f32[136,256]{1,0:T(8,128)S(1)}, u32[]{:S(2)}, u32[]{:S(2)}) collective-permute-start(f32[136,256]{1,0:T(8,128)S(1)} %get-tuple-element.27), channel_id=1, source_target_pairs={{0,16},{8,24},{16,0},{24,8},{32,48},{40,56},{48,32},{56,40},{64,80... | collective-permute-start | bytes 417800 | tf_op jit(solution)/shard_map/ppermute | solution.py:344
  63.7 7.9 %collective-permute-start.12 = (f32[8,256]{1,0:T(8,128)S(1)}, f32[8,256]{1,0:T(8,128)S(1)}, u32[]{:S(2)}, u32[]{:S(2)}) collective-permute-start(f32[8,256]{1,0:T(8,128)S(1)} %get-tuple-element.29), channel_id=1, source_target_pairs={{0,1},{1,2},{2,3},{3,4},{4,5},{5,6},{6,7},{8,9},{9,10},{10,11},{11... | collective-permute-start | bytes 24584 | tf_op jit(solution)/shard_map/ppermute | solution.py:391
  67.8 6.4 %collective-permute-start.13 = (f32[8,256]{1,0:T(8,128)S(1)}, f32[8,256]{1,0:T(8,128)S(1)}, u32[]{:S(2)}, u32[]{:S(2)}) collective-permute-start(f32[8,256]{1,0:T(8,128)S(1)} %get-tuple-element.30), channel_id=1, source_target_pairs={{1,0},{2,1},{3,2},{4,3},{5,4},{6,5},{7,6},{9,8},{10,9},{11,10},{12... | collective-permute-start | bytes 24584 | tf_op jit(solution)/shard_map/ppermute | solution.py:392

commit v5 on v4

--- a/solution.py
+++ b/solution.py
@@ -177,9 +177,9 @@
     prepare(tab[b0], 0, mats, phases, steps)
     prepare(tab[1 - b0], 1, mats, phases, steps)
     prepare(tab[2 + b1], 2, mats, phases, steps)
-    prepare(tabx[2 + b1], 3, mats, phases, steps)
-    for at, ref in ((4, tab), (5, tabx), (6, taby), (7, tabd)):
-        prepare(ref[4 + b2], at, mats, phases, steps)
+    prepare(tabx[b1], 3, mats, phases, steps)
+    for at, ref, first_row in ((4, tab, 4), (5, tabx, 2), (6, taby, 2), (7, tabd, 2)):
+        prepare(ref[first_row + b2], at, mats, phases, steps)
     run = functools.partial(stage, zz=zz, uu=uu, table=table, mats=mats, phases=phases, steps=steps)
 
     def blocks(ref):
@@ -238,7 +238,7 @@
         ref[...] = (g0[k] + r1[k]) + (r2[k] + r3[k])
 
 
-def table_kernel(owners, index, weight, shift, gain, out):
+def table_kernel(owners, index, weight, shift, gain, out, sent):
     lane = lax.broadcasted_iota(jnp.int32, (4, A), 1)
     row = jnp.zeros((4, A), jnp.int32)
     for q in range(8):
@@ -249,6 +249,7 @@
         out[k, 8:16] = weight[section, 0, child]
         out[k, 16:20] = jnp.broadcast_to(shift[section, 0, child : child + 1, :], (4, A))
         out[k, 20:24] = row.astype(F32)
+    sent[...] = out[2:6]
     for section in range(3):
         for k in range(8):
             at = 8 * section + k
@@ -349,10 +350,10 @@
     bits = jnp.stack([place & 1, (place >> 1) & 1, (place >> 2) & 1, place])
     own_weights = weights[0, 0]
     wx, wy, wd = (swap(own_weights, mask) for mask in (2, 4, 6))
-    tab = call(table_kernel, struct((7, 24, A)), [SMEM] + [VMEM] * 4, limit=60)(
+    tab, sent = call(table_kernel, (struct((7, 24, A)), struct((4, 24, A))), [SMEM] + [VMEM] * 4, limit=60)(
         tile_owner.reshape(8), tap_index, tap_weight, range_shift, range_gain
     )
-    tabx, taby, tabd = (swap(tab, mask) for mask in (2, 4, 6))
+    tabx, taby, tabd = (swap(sent, mask) for mask in (2, 4, 6))
     tabx, late = lax.optimization_barrier((tabx, polar))
     other = swap(late, 1)
     cur = call(

time: 76.3 us -> 75.6 us (level)
  transfers between devices with their start and end apart: 14 -> 14, of which waited for: 7 -> 8; matrix products, arithmetic and copies ran while one was open for 1% -> 1% of each run, Pallas kernels for 24% -> 24%
where the time goes in v5:
time: 75.6 us; the launch traced here: 75.2 us
  Pallas kernels  23.5 us (31%)
  waiting for transfers between devices  23.2 us (31%)
  starting transfers between devices  23 us (30%)
  local copies, waits for them, and re-layouts  4.47 us (6%)
  between operations  0.76 us (1%)
    ppermute x12, waiting for transfers between devices, swap(): return lax.ppermute(value, 'aper', [(i, i ^ mask) for i in range(16)])  20.6 us
    ppermute x12, starting transfers between devices, swap(): return lax.ppermute(value, 'aper', [(i, i ^ mask) for i in range(16)])  16.9 us
    pallas_call x1, Pallas kernels, shards(): call(merge_kernel, struct((4, 8, 2 * A, H), BF16), [SMEM] + [VMEM] * 5 +...  16.1 us
    ppermute x1, starting transfers between devices, shards(): before = lax.ppermute(last, 'swath', [(i, i + 1) for i in range(7)])  4.17 us
    unnamed x10, local copies, waits for them, and re-layouts  3.77 us
    ppermute x1, waiting for transfers between devices, shards(): after = lax.ppermute(first, 'swath', [(i + 1, i) for i in range(7)])  2.65 us
    pallas_call x1, Pallas kernels, shards(): call(contrib_kernel, (struct((8, ROWS, H)), struct((8, ROWS, H))), [SMEM,...  2.18 us
    ppermute x1, starting transfers between devices, shards(): after = lax.ppermute(first, 'swath', [(i + 1, i) for i in range(7)])  1.92 us
  transfers between devices with their start and end apart: 14, of which 8 were waited for; matrix products, arithmetic and copies ran while one was open for 1% of the time, Pallas kernels for 24%

profile of v5, /device:TPU:34, one launch (start us, length us, event | category | flops | bytes accessed | tf_op | source)
XLA Modules:
  0.0 75.2 jit_solution(3765161582450788438)
XLA Ops:
  0.0 1.5 %shard_map.100 = (f32[7,24,128]{2,1,0:T(8,128)}, f32[4,24,128]{2,1,0:T(8,128)}) custom-call(s32[8]{0:T(128)} %bitcast.18, s32[3,1,2,8,128]{4,3,2,1,0:T(8,128)} %index.3, f32[3,1,2,8,128]{4,3,2,1,0:T(8,128)} %weight.1, f32[3,1,2,128]{3,2,1,0:T(2,128)} %shift.1, f32[3,1024]{1,0:T(4,128)} %gain.1), custom_call_target="tpu_custom_call" | custom-call | flops 1000000 | bytes 1048576 | tf_op jit(solution)/shard_map/pallas_call | solution.py:353
  1.5 2.1 %collective-permute-start = (f32[4,24,128]{2,1,0:T(8,128)}, f32[4,24,128]{2,1,0:T(8,128)S(1)}, u32[]{:S(2)}, u32[]{:S(2)}) collective-permute-start(f32[4,24,128]{2,1,0:T(8,128)} %get-tuple-element.21), channel_id=1, source_target_pairs={{0,16},{8,24},{16,0},{24,8},{32,48},{40,56},{48,32},{56,40},{64,80... | collective-permute-start | bytes 147464 | tf_op jit(solution)/shard_map/ppermute | solution.py:345
  3.6 1.6 %collective-permute-start.1 = (f32[4,24,128]{2,1,0:T(8,128)}, f32[4,24,128]{2,1,0:T(8,128)S(1)}, u32[]{:S(2)}, u32[]{:S(2)}) collective-permute-start(f32[4,24,128]{2,1,0:T(8,128)} %get-tuple-element.21), channel_id=1, source_target_pairs={{0,32},{8,40},{16,48},{24,56},{32,0},{40,8},{48,16},{56,24},{64,96... | collective-permute-start | bytes 147464 | tf_op jit(solution)/shard_map/ppermute | solution.py:345
  5.2 1.3 %collective-permute-start.2 = (f32[4,24,128]{2,1,0:T(8,128)}, f32[4,24,128]{2,1,0:T(8,128)S(1)}, u32[]{:S(2)}, u32[]{:S(2)}) collective-permute-start(f32[4,24,128]{2,1,0:T(8,128)} %get-tuple-element.21), channel_id=1, source_target_pairs={{0,48},{8,56},{16,32},{24,40},{32,16},{40,24},{48,0},{56,8},{64,11... | collective-permute-start | bytes 147464 | tf_op jit(solution)/shard_map/ppermute | solution.py:345
  6.5 2.1 %collective-permute-start.4 = (f32[8,128,128]{2,1,0:T(8,128)}, f32[8,128,128]{2,1,0:T(8,128)S(1)}, u32[]{:S(2)}, u32[]{:S(2)}) collective-permute-start(f32[8,128,128]{2,1,0:T(8,128)} %bitcast.14), channel_id=1, source_target_pairs={{0,16},{8,24},{16,0},{24,8},{32,48},{40,56},{48,32},{56,40},{64,80... | collective-permute-start | bytes 1572872 | tf_op jit(solution)/shard_map/ppermute | solution.py:345
  8.6 1.6 %collective-permute-start.5 = (f32[8,128,128]{2,1,0:T(8,128)}, f32[8,128,128]{2,1,0:T(8,128)S(1)}, u32[]{:S(2)}, u32[]{:S(2)}) collective-permute-start(f32[8,128,128]{2,1,0:T(8,128)} %bitcast.15), channel_id=1, source_target_pairs={{0,32},{8,40},{16,48},{24,56},{32,0},{40,8},{48,16},{56,24},{64,96... | collective-permute-start | bytes 1572872 | tf_op jit(solution)/shard_map/ppermute | solution.py:345
  10.9 1.4 %collective-permute-done.2.tabd = f32[4,24,128]{2,1,0:T(8,128)S(1)} collective-permute-done((f32[4,24,128]{2,1,0:T(8,128)}, f32[4,24,128]{2,1,0:T(8,128)S(1)}, u32[]{:S(2)}, u32[]{:S(2)}) %collective-permute-start.2) | collective-permute-done | bytes 49184 | tf_op jit(solution)/shard_map/ppermute | solution.py:345
  13.6 1.3 %copy-done.2 = f32[2,128,1024]{2,1,0:T(8,128)S(1)} copy-done((f32[2,128,1024]{2,1,0:T(8,128)S(1)}, f32[2,128,1024]{2,1,0:T(8,128)}, u32[]{:S(2)}) %copy-start.2) | copy-done | bytes 1048600
  15.8 1.6 %copy-done.4 = bf16[2,8,256,256]{3,2,1,0:T(8,128)(2,1)S(1)} copy-done((bf16[2,8,256,256]{3,2,1,0:T(8,128)(2,1)S(1)}, bf16[2,8,256,256]{3,2,1,0:T(8,128)(2,1)}, u32[]{:S(2)}) %copy-start.4) | copy-done | bytes 2097176
  17.4 16.1 %shard_map.101.cur = bf16[4,8,256,256]{3,2,1,0:T(8,128)(2,1)S(1)} custom-call(s32[4]{0:T(128)S(1)} %pad_add_fusion.bits, f32[2,128,1024]{2,1,0:T(8,128)S(1)} %collective-permute-done.3.other, f32[7,24,128]{2,1,0:T(8,128)S(1)} %copy-done.3, f32[4,24,128]{2,1,0:T(8,128)S(1)} %collective-permute-done.tabx, f32[4,24,128]{2,1,0:T(8,128)S(1)} %collective-permute-done.1.taby, ...), custom_call_target="tpu_custom_call" | custom-call | flops 12000000000 | bytes 1048576 | tf_op jit(solution)/shard_map/pallas_call | solution.py:359
  33.8 2.2 %shard_map.102 = (f32[8,136,256]{2,1,0:T(8,128)S(1)}, f32[8,136,256]{2,1,0:T(8,128)S(1)}) custom-call(s32[32]{0:T(128)S(1)} %maximum_convert_fusion.owners, s32[4]{0:T(128)S(1)} %pad_add_fusion.bits, bf16[4,8,256,256]{3,2,1,0:T(8,128)(2,1)S(1)} %shard_map.101.cur, f32[8,128,128]{2,1,0:T(8,128)S(1)} %bitcast.17, ...), custom_call_target="tpu_custom_call" | custom-call | flops 1000000000 | bytes 1048576 | tf_op jit(solution)/shard_map/pallas_call | solution.py:377
  36.1 2.7 %collective-permute-done.7.taken = f32[8,136,256]{2,1,0:T(8,128)S(1)} collective-permute-done((f32[8,136,256]{2,1,0:T(8,128)S(1)}, f32[8,136,256]{2,1,0:T(8,128)S(1)}, u32[]{:S(2)}, u32[]{:S(2)}) %collective-permute-start.7) | collective-permute-done | bytes 1114144 | tf_op jit(solution)/shard_map/ppermute | solution.py:345
  39.0 2.9 %collective-permute-start.10 = (f32[2,136,256]{2,1,0:T(8,128)S(1)}, f32[2,136,256]{2,1,0:T(8,128)S(1)}, u32[]{:S(2)}, u32[]{:S(2)}) collective-permute-start(f32[2,136,256]{2,1,0:T(8,128)S(1)} %get-tuple-element.29), channel_id=1, source_target_pairs={{0,96},{8,104},{16,112},{24,120},{32,64},{40,72},{48,80},{56,88},{... | collective-permute-start | bytes 835592 | tf_op jit(solution)/shard_map/ppermute | solution.py:345
  42.0 1.8 %collective-permute-start.9 = (f32[2,136,256]{2,1,0:T(8,128)S(1)}, f32[2,136,256]{2,1,0:T(8,128)S(1)}, u32[]{:S(2)}, u32[]{:S(2)}) collective-permute-start(f32[2,136,256]{2,1,0:T(8,128)S(1)} %get-tuple-element.28), channel_id=1, source_target_pairs={{0,64},{8,72},{16,80},{24,88},{32,96},{40,104},{48,112},{56,120},{... | collective-permute-start | bytes 835592 | tf_op jit(solution)/shard_map/ppermute | solution.py:345
  43.7 5.2 %collective-permute-done.10.r3 = f32[2,136,256]{2,1,0:T(8,128)S(1)} collective-permute-done((f32[2,136,256]{2,1,0:T(8,128)S(1)}, f32[2,136,256]{2,1,0:T(8,128)S(1)}, u32[]{:S(2)}, u32[]{:S(2)}) %collective-permute-start.10) | collective-permute-done | bytes 278560 | tf_op jit(solution)/shard_map/ppermute | solution.py:345
  48.9 2.4 %collective-permute-done.8.r1 = f32[2,136,256]{2,1,0:T(8,128)S(1)} collective-permute-done((f32[2,136,256]{2,1,0:T(8,128)S(1)}, f32[2,136,256]{2,1,0:T(8,128)S(1)}, u32[]{:S(2)}, u32[]{:S(2)}) %collective-permute-start.8) | collective-permute-done | bytes 278560 | tf_op jit(solution)/shard_map/ppermute | solution.py:345
  51.4 4.7 %collective-permute-done.9.r2 = f32[2,136,256]{2,1,0:T(8,128)S(1)} collective-permute-done((f32[2,136,256]{2,1,0:T(8,128)S(1)}, f32[2,136,256]{2,1,0:T(8,128)S(1)}, u32[]{:S(2)}, u32[]{:S(2)}) %collective-permute-start.9) | collective-permute-done | bytes 278560 | tf_op jit(solution)/shard_map/ppermute | solution.py:345
  56.2 2.2 %collective-permute-start.11 = (f32[136,256]{1,0:T(8,128)S(1)}, f32[136,256]{1,0:T(8,128)S(1)}, u32[]{:S(2)}, u32[]{:S(2)}) collective-permute-start(f32[136,256]{1,0:T(8,128)S(1)} %get-tuple-element.31), channel_id=1, source_target_pairs={{0,16},{8,24},{16,0},{24,8},{32,48},{40,56},{48,32},{56,40},{64,80... | collective-permute-start | bytes 417800 | tf_op jit(solution)/shard_map/ppermute | solution.py:345
  59.0 3.8 %collective-permute-done.11.taken = f32[136,256]{1,0:T(8,128)S(1)} collective-permute-done((f32[136,256]{1,0:T(8,128)S(1)}, f32[136,256]{1,0:T(8,128)S(1)}, u32[]{:S(2)}, u32[]{:S(2)}) %collective-permute-start.11) | collective-permute-done | bytes 139296 | tf_op jit(solution)/shard_map/ppermute | solution.py:345
  63.0 4.2 %collective-permute-start.12 = (f32[8,256]{1,0:T(8,128)S(1)}, f32[8,256]{1,0:T(8,128)S(1)}, u32[]{:S(2)}, u32[]{:S(2)}) collective-permute-start(f32[8,256]{1,0:T(8,128)S(1)} %get-tuple-element.33), channel_id=1, source_target_pairs={{0,1},{1,2},{2,3},{3,4},{4,5},{5,6},{6,7},{8,9},{9,10},{10,11},{11... | collective-permute-start | bytes 24584 | tf_op jit(solution)/shard_map/ppermute | solution.py:392
  67.2 1.9 %collective-permute-start.13 = (f32[8,256]{1,0:T(8,128)S(1)}, f32[8,256]{1,0:T(8,128)S(1)}, u32[]{:S(2)}, u32[]{:S(2)}) collective-permute-start(f32[8,256]{1,0:T(8,128)S(1)} %get-tuple-element.34), channel_id=1, source_target_pairs={{1,0},{2,1},{3,2},{4,3},{5,4},{6,5},{7,6},{9,8},{10,9},{11,10},{12... | collective-permute-start | bytes 24584 | tf_op jit(solution)/shard_map/ppermute | solution.py:393
  69.1 1.8 %shard_map.106.main = f32[2,128,128]{2,1,0:T(8,128)S(1)} custom-call(s32[1,1]{1,0:T(1,128)S(6)} %copy.11.index, f32[16,81]{1,0:T(8,128)S(1)} %copy-done.1, f32[136,256]{1,0:T(8,128)S(1)} %get-tuple-element.32.tile), custom_call_target="tpu_custom_call" | custom-call | flops 1000000000 | bytes 1048576 | tf_op jit(solution)/shard_map/pallas_call | solution.py:394
  71.0 2.7 %collective-permute-done.13.after = f32[8,256]{1,0:T(8,128)S(1)} collective-permute-done((f32[8,256]{1,0:T(8,128)S(1)}, f32[8,256]{1,0:T(8,128)S(1)}, u32[]{:S(2)}, u32[]{:S(2)}) %collective-permute-start.13) | collective-permute-done | bytes 8224 | tf_op jit(solution)/shard_map/ppermute | solution.py:393
  73.6 1.6 %shard_map.107 = f32[2,128,128]{2,1,0:T(8,128)} custom-call(s32[1,1]{1,0:T(1,128)S(6)} %copy.11.index, f32[16,81]{1,0:T(8,128)S(1)} %copy-done.1, f32[2,128,128]{2,1,0:T(8,128)S(1)} %shard_map.106.main, f32[8,256]{1,0:T(8,128)S(1)} %collective-permute-done.12.before, f32[8,256]{1,0:T(8,128)S(1)} %collective-permute-done.13.after), custom_call_target="tpu_custom_call" | custom-call | flops 1000000 | bytes 1048576 | tf_op jit(solution)/shard_map/pallas_call | solution.py:405
  (28 shorter events, 3.9 us)
Async XLA Ops:
  1.5 8.7 %collective-permute-start = (f32[4,24,128]{2,1,0:T(8,128)}, f32[4,24,128]{2,1,0:T(8,128)S(1)}, u32[]{:S(2)}, u32[]{:S(2)}) collective-permute-start(f32[4,24,128]{2,1,0:T(8,128)} %get-tuple-element.21), channel_id=1, source_target_pairs={{0,16},{8,24},{16,0},{24,8},{32,48},{40,56},{48,32},{56,40},{64,80... | collective-permute-start | bytes 147464 | tf_op jit(solution)/shard_map/ppermute | solution.py:345
  3.6 10.0 %collective-permute-start.1 = (f32[4,24,128]{2,1,0:T(8,128)}, f32[4,24,128]{2,1,0:T(8,128)S(1)}, u32[]{:S(2)}, u32[]{:S(2)}) collective-permute-start(f32[4,24,128]{2,1,0:T(8,128)} %get-tuple-element.21), channel_id=1, source_target_pairs={{0,32},{8,40},{16,48},{24,56},{32,0},{40,8},{48,16},{56,24},{64,96... | collective-permute-start | bytes 147464 | tf_op jit(solution)/shard_map/ppermute | solution.py:345
  5.2 7.2 %collective-permute-start.2 = (f32[4,24,128]{2,1,0:T(8,128)}, f32[4,24,128]{2,1,0:T(8,128)S(1)}, u32[]{:S(2)}, u32[]{:S(2)}) collective-permute-start(f32[4,24,128]{2,1,0:T(8,128)} %get-tuple-element.21), channel_id=1, source_target_pairs={{0,48},{8,56},{16,32},{24,40},{32,16},{40,24},{48,0},{56,8},{64,11... | collective-permute-start | bytes 147464 | tf_op jit(solution)/shard_map/ppermute | solution.py:345
  6.5 27.0 %collective-permute-start.4 = (f32[8,128,128]{2,1,0:T(8,128)}, f32[8,128,128]{2,1,0:T(8,128)S(1)}, u32[]{:S(2)}, u32[]{:S(2)}) collective-permute-start(f32[8,128,128]{2,1,0:T(8,128)} %bitcast.14), channel_id=1, source_target_pairs={{0,16},{8,24},{16,0},{24,8},{32,48},{40,56},{48,32},{56,40},{64,80... | collective-permute-start | bytes 1572872 | tf_op jit(solution)/shard_map/ppermute | solution.py:345
  8.6 24.9 %collective-permute-start.5 = (f32[8,128,128]{2,1,0:T(8,128)}, f32[8,128,128]{2,1,0:T(8,128)S(1)}, u32[]{:S(2)}, u32[]{:S(2)}) collective-permute-start(f32[8,128,128]{2,1,0:T(8,128)} %bitcast.15), channel_id=1, source_target_pairs={{0,32},{8,40},{16,48},{24,56},{32,0},{40,8},{48,16},{56,24},{64,96... | collective-permute-start | bytes 1572872 | tf_op jit(solution)/shard_map/ppermute | solution.py:345
  10.2 3.5 %collective-permute-start.3 = (f32[2,128,1024]{2,1,0:T(8,128)}, f32[2,128,1024]{2,1,0:T(8,128)S(1)}, u32[]{:S(2)}, u32[]{:S(2)}) collective-permute-start(f32[2,128,1024]{2,1,0:T(8,128)} %own_in.1), channel_id=1, source_target_pairs={{0,8},{8,0},{16,24},{24,16},{32,40},{40,32},{48,56},{56,48},{64,72... | collective-permute-start | bytes 3145736 | tf_op jit(solution)/shard_map/ppermute | solution.py:345
  12.3 21.4 %collective-permute-start.6 = (f32[8,128,128]{2,1,0:T(8,128)}, f32[8,128,128]{2,1,0:T(8,128)S(1)}, u32[]{:S(2)}, u32[]{:S(2)}) collective-permute-start(f32[8,128,128]{2,1,0:T(8,128)} %bitcast.16), channel_id=1, source_target_pairs={{0,48},{8,56},{16,32},{24,40},{32,16},{40,24},{48,0},{56,8},{64,11... | collective-permute-start | bytes 1572872 | tf_op jit(solution)/shard_map/ppermute | solution.py:345
  13.6 20.1 %copy-start = (f32[1,1,8,128,128]{4,3,2,1,0:T(8,128)S(1)}, f32[1,1,8,128,128]{4,3,2,1,0:T(8,128)}, u32[]{:S(2)}) copy-start(f32[1,1,8,128,128]{4,3,2,1,0:T(8,128)} %param.16) | copy-start | bytes 1572868
  13.6 1.3 %copy-start.2 = (f32[2,128,1024]{2,1,0:T(8,128)S(1)}, f32[2,128,1024]{2,1,0:T(8,128)}, u32[]{:S(2)}) copy-start(f32[2,128,1024]{2,1,0:T(8,128)} %own_in.1) | copy-start | bytes 3145732
  14.9 0.9 %copy-start.3 = (f32[7,24,128]{2,1,0:T(8,128)S(1)}, f32[7,24,128]{2,1,0:T(8,128)}, u32[]{:S(2)}) copy-start(f32[7,24,128]{2,1,0:T(8,128)} %get-tuple-element.20.tab) | copy-start | bytes 258052
  15.8 1.6 %copy-start.4 = (bf16[2,8,256,256]{3,2,1,0:T(8,128)(2,1)S(1)}, bf16[2,8,256,256]{3,2,1,0:T(8,128)(2,1)}, u32[]{:S(2)}) copy-start(bf16[2,8,256,256]{3,2,1,0:T(8,128)(2,1)} %constant.12.clone.table_in) | copy-start | bytes 6291460
  36.0 2.8 %collective-permute-start.7 = (f32[8,136,256]{2,1,0:T(8,128)S(1)}, f32[8,136,256]{2,1,0:T(8,128)S(1)}, u32[]{:S(2)}, u32[]{:S(2)}) collective-permute-start(f32[8,136,256]{2,1,0:T(8,128)S(1)} %get-tuple-element.25), channel_id=1, source_target_pairs={{0,8},{8,0},{16,24},{24,16},{32,40},{40,32},{48,56},{56,48},{64,72... | collective-permute-start | bytes 3342344 | tf_op jit(solution)/shard_map/ppermute | solution.py:345
  38.9 30.2 %copy-start.1 = (f32[16,81]{1,0:T(8,128)S(1)}, f32[16,81]{1,0:T(8,128)}, u32[]{:S(2)}) copy-start(f32[16,81]{1,0:T(8,128)} %bank.3) | copy-start | bytes 15556
  39.0 10.0 %collective-permute-start.10 = (f32[2,136,256]{2,1,0:T(8,128)S(1)}, f32[2,136,256]{2,1,0:T(8,128)S(1)}, u32[]{:S(2)}, u32[]{:S(2)}) collective-permute-start(f32[2,136,256]{2,1,0:T(8,128)S(1)} %get-tuple-element.29), channel_id=1, source_target_pairs={{0,96},{8,104},{16,112},{24,120},{32,64},{40,72},{48,80},{56,88},{... | collective-permute-start | bytes 835592 | tf_op jit(solution)/shard_map/ppermute | solution.py:345
  41.8 9.5 %collective-permute-start.8 = (f32[2,136,256]{2,1,0:T(8,128)S(1)}, f32[2,136,256]{2,1,0:T(8,128)S(1)}, u32[]{:S(2)}, u32[]{:S(2)}) collective-permute-start(f32[2,136,256]{2,1,0:T(8,128)S(1)} %get-tuple-element.27), channel_id=1, source_target_pairs={{0,32},{8,40},{16,48},{24,56},{32,0},{40,8},{48,16},{56,24},{64,96... | collective-permute-start | bytes 835592 | tf_op jit(solution)/shard_map/ppermute | solution.py:345
  42.0 14.1 %collective-permute-start.9 = (f32[2,136,256]{2,1,0:T(8,128)S(1)}, f32[2,136,256]{2,1,0:T(8,128)S(1)}, u32[]{:S(2)}, u32[]{:S(2)}) collective-permute-start(f32[2,136,256]{2,1,0:T(8,128)S(1)} %get-tuple-element.28), channel_id=1, source_target_pairs={{0,64},{8,72},{16,80},{24,88},{32,96},{40,104},{48,112},{56,120},{... | collective-permute-start | bytes 835592 | tf_op jit(solution)/shard_map/ppermute | solution.py:345
  56.2 6.6 %collective-permute-start.11 = (f32[136,256]{1,0:T(8,128)S(1)}, f32[136,256]{1,0:T(8,128)S(1)}, u32[]{:S(2)}, u32[]{:S(2)}) collective-permute-start(f32[136,256]{1,0:T(8,128)S(1)} %get-tuple-element.31), channel_id=1, source_target_pairs={{0,16},{8,24},{16,0},{24,8},{32,48},{40,56},{48,32},{56,40},{64,80... | collective-permute-start | bytes 417800 | tf_op jit(solution)/shard_map/ppermute | solution.py:345
  63.0 8.0 %collective-permute-start.12 = (f32[8,256]{1,0:T(8,128)S(1)}, f32[8,256]{1,0:T(8,128)S(1)}, u32[]{:S(2)}, u32[]{:S(2)}) collective-permute-start(f32[8,256]{1,0:T(8,128)S(1)} %get-tuple-element.33), channel_id=1, source_target_pairs={{0,1},{1,2},{2,3},{3,4},{4,5},{5,6},{6,7},{8,9},{9,10},{10,11},{11... | collective-permute-start | bytes 24584 | tf_op jit(solution)/shard_map/ppermute | solution.py:392
  67.2 6.4 %collective-permute-start.13 = (f32[8,256]{1,0:T(8,128)S(1)}, f32[8,256]{1,0:T(8,128)S(1)}, u32[]{:S(2)}, u32[]{:S(2)}) collective-permute-start(f32[8,256]{1,0:T(8,128)S(1)} %get-tuple-element.34), channel_id=1, source_target_pairs={{1,0},{2,1},{3,2},{4,3},{5,4},{6,5},{7,6},{9,8},{10,9},{11,10},{12... | collective-permute-start | bytes 24584 | tf_op jit(solution)/shard_map/ppermute | solution.py:393
